TPU v7x, 32 devices: a whole 2x2x4 slice. The times are simulated.
32 devices in a mesh: ka: 16 (over z, y, core), band: 2 (over x).
Axes of the slice: x: 2, y: 2, z: 4, core: 2. Of those that a mesh axis runs over, the one named last changes fastest.
Arguments:
- coefficients: bfloat16 [16, 2, 40, 2400], P('ka'), may hold values from -6 to 6
- class_weight: float32 [16], replicated, may hold values from 0.5 to 5
- diff_class: int32 [16, 16], replicated, may hold values from 0 to 15
- frag_cells: int32 [2], replicated, may hold values from 0 to 15
- block_pattern: int32 [2, 30], replicated, may hold values 0 or 1
Outputs:
- cluster: float32 [2, 2, 40, 2400], P(None, None, 'band', 'ka')
All inputs are finite; a program needn't handle non-finite values.
Results may differ from a plain program's by a relative error of at most 0.0017.
Values may be sent and summed in bfloat16 or wider, within the bound.
A program may use at most 64 MiB of HBM per device.

v0:
```python
import jax
import jax.numpy as jnp
from jax import lax
from jax.sharding import PartitionSpec as P


def shards(coefficients, class_weight, diff_class, frag_cells, block_pattern):
    own_block = coefficients[0]
    occupied = own_block.shape[1]
    functions = own_block.shape[2]
    band_count = lax.axis_size("band")
    group_width = occupied // band_count
    kpoint_count = lax.axis_size("ka")
    kpoint_index = lax.axis_index("ka")
    high = lax.Precision.HIGHEST
    own_flat = own_block.reshape(2 * occupied, functions)
    my_group = lax.dynamic_slice_in_dim(
        own_block, lax.axis_index("band") * group_width, group_width, 1
    )
    diff_row = lax.dynamic_index_in_dim(diff_class, kpoint_index, 0, keepdims=False)
    classes = jnp.arange(class_weight.shape[0], dtype=jnp.int32)
    onehot = (diff_row[:, None] == classes[None, :]).astype(jnp.float32)
    weights = jnp.dot(onehot, class_weight, precision=high) / functions
    piece = lax.all_gather(my_group[None], "ka", axis=0, tiled=True)
    pieces = piece.shape[0]
    blocks = piece.reshape(pieces, 2 * group_width, functions)
    intersection = jnp.einsum("qia,ja->qij", blocks, own_flat, preferred_element_type=jnp.float32)
    m_real = intersection[:, :group_width, :occupied] + intersection[:, group_width:, occupied:]
    m_imag = intersection[:, :group_width, occupied:] - intersection[:, group_width:, :occupied]
    scaling = weights[:, None, None]
    m_real = (scaling * m_real).astype(jnp.bfloat16)
    m_imag = (scaling * m_imag).astype(jnp.bfloat16)
    m_block = jnp.concatenate(
        [jnp.concatenate([m_real, m_imag], 2), jnp.concatenate([-m_imag, m_real], 2)], 1
    )
    exchange = jnp.einsum("qio,qia->oa", m_block, blocks, preferred_element_type=jnp.float32)
    exchange = exchange.reshape(2, occupied, functions)
    phase_index = kpoint_index * frag_cells % kpoint_count
    angles = 2.0 * jnp.pi * phase_index.astype(jnp.float32) / kpoint_count
    cosines = (jnp.cos(angles) / kpoint_count)[:, None, None]
    sines = (jnp.sin(angles) / kpoint_count)[:, None, None]
    w_real = exchange[0][None]
    w_imag = exchange[1][None]
    terms = jnp.stack([cosines * w_real - sines * w_imag, sines * w_real + cosines * w_imag], 1)
    partial_value = lax.psum_scatter(terms, "band", scatter_dimension=2, tiled=True)
    cluster = lax.psum_scatter(partial_value, "ka", scatter_dimension=3, tiled=True)
    columns = cluster.shape[3]
    block_size = functions // block_pattern.shape[1]
    local_ids = (kpoint_index * columns + jnp.arange(columns, dtype=jnp.int32)) // block_size
    block_ids = jnp.arange(block_pattern.shape[1], dtype=jnp.int32)
    block_onehot = (block_ids[:, None] == local_ids[None, :]).astype(jnp.float32)
    block_mask = jnp.dot(block_pattern.astype(jnp.float32), block_onehot, precision=high)
    return cluster * block_mask[:, None, None, :]


def solution(mesh):
    placed = (P("ka", None, None, None), P(), P(), P(), P())
    return jax.shard_map(
        shards, mesh=mesh, in_specs=placed, out_specs=P(None, None, "band", "ka"), check_vma=False
    )
```

profile of v0, /device:TPU:0, one launch (start us, length us, event | category | flops | bytes accessed | tf_op | source)
XLA Modules:
  0.0 219.4 jit_solution(11518755130663620419)
XLA Ops:
  6.5 0.0 copy-start
  6.5 0.0 all-gather.2.cloned.1.call-start
  6.5 1.0 copy-done
  7.5 0.1 constant_dynamic-slice_fusion.1
  7.6 0.8 copy.17
  8.4 0.0 all-gather.2.cloned.1.call-update
  8.4 0.0 all-reduce.5.cloned.1.call-start
  8.5 0.7 dynamic-slice_bitcast_fusion
  9.2 0.7 cosine_multiply_fusion
  9.9 0.8 fusion.3
  10.8 46.6 %all-gather.2.cloned.1.call-done = bf16[16,2,20,2400]{3,1,2,0:T(2,128)(2,1)} async-done(((bf16[1,2,20,2400]{3,1,2,0:T(2,128)(2,1)}), bf16[16,2,20,2400]{3,1,2,0:T(2,128)(2,1)}) %all-gather.2.cloned.1.call-update) | async-done | bytes 3072016 | tf_op jit(solution)/shard_map/all_gather | solution.py:24
  57.4 2.2 %copy.10 = bf16[16,2,20,2400]{3,0,2,1:T(8,128)(2,1)S(1)} copy(bf16[16,2,20,2400]{3,1,2,0:T(2,128)(2,1)} %all-gather.2.cloned.1.call-done) | data formatting | bytes 6144000 | tf_op jit(solution)/shard_map/all_gather | solution.py:24
  59.6 1.0 fusion.1
  60.5 0.1 fusion.7
  60.7 0.1 fusion.24
  60.8 0.8 convolution_bitcast_fusion
  61.7 0.1 fusion.26
  61.7 0.0 copy-start.3
  61.8 1.4 multiply_subtract_fusion
  63.1 0.0 copy-start.2
  63.1 0.0 copy-start.1
  63.1 2.6 %pad_maximum_fusion = f32[2,2,40,2400]{3,1,2,0:T(2,128)} fusion(f32[2,1,40,2400]{3,1,2,0:T(1,128)S(1)} %get-tuple-element.10, f32[2,1,40,2400]{3,1,2,0:T(1,128)S(1)} %get-tuple-element.9), kind=kLoop, calls=%fused_computation.4 | loop fusion | flops 384000 | bytes 3072000 | tf_op jit(solution)/shard_map/stack | solution.py:44
  65.7 0.0 all-reduce.5.cloned.1.call-update
  65.7 0.0 all-reduce.7.cloned.1.call-start
  65.8 0.0 copy-done.3
  65.8 0.6 dynamic-slice.1
  67.0 48.7 %all-reduce.5.cloned.1.call-done = f32[2,2,40,2400]{3,1,2,0:T(2,128)} async-done(((f32[2,2,40,2400]{3,1,2,0:T(2,128)}), f32[2,2,40,2400]{3,1,2,0:T(2,128)}) %all-reduce.5.cloned.1.call-update) | async-done | bytes 1536016
  115.7 2.1 constant_dynamic-slice_fusion
  117.8 0.0 all-reduce.7.cloned.1.call-update
  117.8 0.0 copy-done.2
  117.8 0.6 dynamic-slice.3
  119.1 0.0 copy-done.1
  119.1 0.1 convolution_bitcast_fusion.1
  119.2 91.9 %all-reduce.7.cloned.1.call-done = f32[2,2,20,2400]{3,1,2,0:T(2,128)} async-done(((f32[2,2,20,2400]{3,1,2,0:T(2,128)}), f32[2,2,20,2400]{3,1,2,0:T(2,128)}) %all-reduce.7.cloned.1.call-update) | async-done | bytes 768016
  211.2 1.7 dynamic-slice_multiply_fusion
  (2 shorter events, 0.1 us)
Async XLA Ops:
  6.5 1.0 copy-start
  6.5 50.8 %all-gather.2.cloned.1.call-start = ((), (), s32[]{:S(2)}) async-start(), calls=%async_computation | async-start | bytes 3307520 | tf_op jit(solution)/shard_map/all_gather | solution.py:24
  8.4 107.3 %all-reduce.5.cloned.1.call-start = ((), (), s32[]{:S(2)}) async-start(), calls=%async_computation.1 | async-start | bytes 3112960
  61.7 4.0 %copy-start.3 = (u32[32]{0:T(128)S(1)}, u32[32]{0:T(128)}, u32[]{:S(2)}) copy-start(u32[32]{0:T(128)} %constant.59) | copy-start | bytes 388
  63.1 54.7 %copy-start.2 = (u32[32]{0:T(128)S(1)}, u32[32]{0:T(128)}, u32[]{:S(2)}) copy-start(u32[32]{0:T(128)} %constant.63) | copy-start | bytes 388
  63.1 56.0 %copy-start.1 = (s32[2,30]{1,0:T(2,128)S(1)}, s32[2,30]{1,0:T(2,128)}, u32[]{:S(2)}) copy-start(s32[2,30]{1,0:T(2,128)} %param.9) | copy-start | bytes 724
  65.7 145.5 %all-reduce.7.cloned.1.call-start = ((), (), s32[]{:S(2)}) async-start(), calls=%async_computation.2 | async-start | bytes 1556480
Sparse Core Ops, SparseCore 0:
  9.5 47.8 all-gather.1
  65.8 49.8 all-reduce.4
  119.1 91.9 all-reduce.6
where the time goes:
time: 220 us; the launch traced here: 219 us
  waiting for transfers between devices  187 us (85%)
  between operations  14.5 us (7%)
  local copies, waits for them, and re-layouts  8.09 us (4%)
  other arithmetic  6.64 us (3%)
  matrix products  2.78 us (1%)
    unnamed x5, waiting for transfers between devices  141 us
    all_gather x1, waiting for transfers between devices, shards(): piece = lax.all_gather(my_group[None], 'ka', axis=0, tiled=True)  46.6 us
    unnamed x12, local copies, waits for them, and re-layouts  5.08 us
  transfers between devices with their start and end apart: 3, of which 3 were waited for; matrix products, arithmetic and copies ran while one was open for 2% of the time, Pallas kernels for 0%

commit v1 on v0

v1 whole, which is shorter than its diff:
```python
import functools
import math

import jax
import jax.numpy as jnp
from jax import lax
from jax.experimental import pallas as pl
from jax.experimental.pallas import tpu as pltpu
from jax.sharding import PartitionSpec as P

MESH = pl.DeviceIdType.MESH
LANES = 128
ROWS = 24
PAIR = 2 * ROWS
STRIDE = 32
SLOT = 64


def kernel(nk, bands, width, occupied, functions, blocks, cells,
           own, weight, classes, frag, pattern, out,
           sel, slots, stack, acc, acc_in, packed, part, part_in,
           right_s, right_r, left_s, left_r, win_s, win_r, gat_s, gat_r, one_s, one_r):
    n = nk // 2
    half = n // 2
    ka, band = lax.axis_index("ka"), lax.axis_index("band")
    chip, core = ka // 2, ka % 2
    padded = slots.shape[2]
    tiles = padded // LANES
    first = (tiles + 1) // 2 * LANES
    chunks = (pl.ds(0, first), pl.ds(first, padded - first))
    window = stack.shape[3]
    columns = functions // nk
    lanes = 2 * bands * STRIDE

    def chip_at(ring):
        return jnp.where(ring < half, 2 * ring, 2 * (n - 1 - ring) + 1)

    row, odd = chip // 2, chip % 2
    ring = jnp.where(odd == 0, row, n - 1 - row)

    def member(offset):
        return 2 * chip_at((ring + offset + n) % n) + core

    sibling = 2 * chip + 1 - core
    barrier = pltpu.get_barrier_semaphore()
    for offset in range(1, n):
        pl.semaphore_signal(barrier, inc=1, device_id=(member(offset), band), device_id_type=MESH)
    pl.semaphore_signal(barrier, inc=1, device_id=(sibling, band), device_id_type=MESH)
    for offset in range(1, bands):
        pl.semaphore_signal(barrier, inc=1, device_id=(ka, (band + offset) % bands), device_id_type=MESH)

    def pick(rows, target):
        r = lax.broadcasted_iota(jnp.int32, (rows, occupied), 0)
        c = lax.broadcasted_iota(jnp.int32, (rows, occupied), 1)
        return target(r, c).astype(jnp.bfloat16)

    def dot(a, b):
        return jnp.dot(a, b, preferred_element_type=jnp.float32)

    re, im = own[0, 0], own[0, 1]
    pick_re = pick(PAIR, lambda r, c: jnp.where((r < width) & (c == r + band * width), 1.0, 0.0))
    pick_im = pick(PAIR, lambda r, c: jnp.where(
        (r >= ROWS) & (r < ROWS + width) & (c == r - ROWS + band * width), 1.0, 0.0))
    slots[0, :, padded - LANES:] = jnp.zeros((PAIR, LANES), jnp.bfloat16)
    slots[0, :, :functions] = (dot(pick_re, re) + dot(pick_im, im)).astype(jnp.bfloat16)

    def group_pick(r, c):
        hit = jnp.zeros(r.shape, jnp.float32)
        for g in range(bands):
            low = ((band - g + bands) % bands) * width
            inside = (r >= g * STRIDE) & (r < g * STRIDE + width)
            hit = jnp.where(inside & (c - low == r - g * STRIDE), 1.0, hit)
        return hit

    pl.semaphore_wait(barrier, n - 1 + 1 + bands - 1)

    def ring_copy(to_right, s, h):
        if to_right:
            src, dst, ss, rs, to = s - 1, s, right_s, right_r, member(1)
        else:
            src, dst, ss, rs, to = (n - s + 1) % n, n - s, left_s, left_r, member(-1)
        return pltpu.make_async_remote_copy(
            src_ref=slots.at[src, :, chunks[h]], dst_ref=slots.at[dst, :, chunks[h]],
            send_sem=ss.at[s - 1, h], recv_sem=rs.at[s - 1, h],
            device_id=(to, band), device_id_type=MESH)

    def has(to_right, s, h):
        return s < half or (s == half and h == (0 if to_right else 1))

    start = pl.multiple_of(jnp.minimum(chip * 2 * columns // LANES, tiles - window // LANES) * LANES, LANES)

    def window_copy(g, t):
        return pltpu.make_async_remote_copy(
            src_ref=slots.at[t, :, pl.ds(start, window)], dst_ref=stack.at[t, g, pl.ds(0, PAIR), :],
            send_sem=win_s.at[g - 1, t], recv_sem=win_r.at[g - 1, t],
            device_id=(ka, (band + g) % bands), device_id_type=MESH)

    def spread(t):
        for g in range(1, bands):
            window_copy(g, t).start()
        stack[t, 0, 0:PAIR, :] = slots[t, :, pl.ds(start, window)]

    for h in range(2):
        for side in (True, False):
            if has(side, 1, h):
                ring_copy(side, 1, h).start()

    groups = pick(bands * STRIDE, group_pick)
    for ri, value in enumerate((re, im)):
        sel[core, ri, :, padded - LANES:] = jnp.zeros((bands * STRIDE, LANES), jnp.bfloat16)
        sel[core, ri, :, :functions] = dot(groups, value).astype(jnp.bfloat16)
    sel_copy = pltpu.make_async_remote_copy(
        src_ref=sel.at[core], dst_ref=sel.at[core], send_sem=one_s.at[0], recv_sem=one_r.at[0],
        device_id=(sibling, band), device_id_type=MESH)
    sel_copy.start()
    stack[:, :, PAIR:, :] = jnp.zeros((n, bands, SLOT - PAIR, window), jnp.bfloat16)
    spread(0)

    at = lax.broadcasted_iota(jnp.int32, (n, lanes), 0)
    where = ring - at
    where = jnp.where(where < 0, where + n, where)
    kpoint = (2 * chip_at(where) + core).astype(jnp.float32)
    cosines, sines = [], []
    for f in range(cells):
        turns = kpoint * (frag[f].astype(jnp.float32) / nk)
        angle = 2.0 * math.pi * (turns - jnp.floor(turns))
        cosines.append(jnp.cos(angle) / nk)
        sines.append(jnp.sin(angle) / nk)
    wide = (columns + LANES - 1) // LANES * LANES
    column = lax.broadcasted_iota(jnp.int32, (ROWS, wide), 1) + ka * columns
    block = functions // blocks
    masks = []
    for f in range(cells):
        mask = jnp.zeros((ROWS, wide), jnp.float32)
        for i in range(blocks):
            keep = (column >= i * block) & (column < (i + 1) * block)
            mask = jnp.where(keep, pattern[f, i].astype(jnp.float32), mask)
        masks.append(mask)

    lane = lax.broadcasted_iota(jnp.int32, (ROWS, lanes), 1)
    lane_core = lane // (lanes // 2)

    def overlap(t):
        k = member(-t)
        block_k = slots[t]
        pieces = []
        for ri in range(2):
            cols = [lax.dot_general(block_k, sel[c, ri], (((1,), (1,)), ((), ())),
                                    preferred_element_type=jnp.float32) for c in range(2)]
            pieces.append(jnp.concatenate(cols, 1))
        by_re, by_im = pieces
        m_real = by_re[:ROWS] + by_im[ROWS:]
        m_imag = by_re[ROWS:] - by_im[:ROWS]
        scale = jnp.where(lane_core == 0, weight[classes[k, 2 * chip]], weight[classes[k, 2 * chip + 1]])
        scale = scale / functions
        m_real = (scale * m_real).astype(jnp.bfloat16).astype(jnp.float32)
        m_imag = (scale * m_imag).astype(jnp.bfloat16).astype(jnp.float32)
        for f in range(cells):
            co, si = cosines[f][t:t + 1], sines[f][t:t + 1]
            a, b = co * m_real - si * m_imag, si * m_real + co * m_imag
            for ri, value in enumerate((a, b)):
                spot = pl.ds((2 * f + ri) * ROWS, ROWS)
                if t == 0:
                    acc[spot, :] = value
                else:
                    acc[spot, :] += value

    sel_copy.wait()
    overlap(0)
    for s in range(1, half + 1):
        for h in range(2):
            for side in (True, False):
                if has(side, s, h):
                    ring_copy(side, s, h).wait_recv()
                    if has(side, s + 1, h):
                        ring_copy(side, s + 1, h).start()
        spread(s)
        if s < half:
            spread(n - s)
        overlap(s)
        if s < half:
            overlap(n - s)

    acc_copy = pltpu.make_async_remote_copy(
        src_ref=acc, dst_ref=acc_in, send_sem=one_s.at[1], recv_sem=one_r.at[1],
        device_id=(sibling, band), device_id_type=MESH)
    acc_copy.start()
    acc_copy.wait_recv()
    total = acc[...] + acc_in[...]
    total = jnp.where(core == 0, total, pltpu.roll(total, lanes // 2, 1))
    for f in range(cells):
        n_re = total[2 * f * ROWS:(2 * f + 1) * ROWS]
        n_im = total[(2 * f + 1) * ROWS:(2 * f + 2) * ROWS]
        value = jnp.zeros((ROWS, lanes), jnp.float32)
        for g in range(bands):
            low = g * SLOT
            a = n_re if g == 0 else pltpu.roll(n_re, g * (SLOT - STRIDE), 1)
            b = pltpu.roll(n_im, g * (SLOT - STRIDE) + ROWS, 1)
            value = jnp.where((lane >= low) & (lane < low + ROWS), a, value)
            value = jnp.where((lane >= low + ROWS) & (lane < low + PAIR), -b, value)
        packed[0, f * ROWS:(f + 1) * ROWS, :] = value

    def gather_copy(t):
        return pltpu.make_async_remote_copy(
            src_ref=packed.at[0], dst_ref=packed.at[t], send_sem=gat_s.at[t - 1], recv_sem=gat_r.at[t - 1],
            device_id=(member(t), band), device_id_type=MESH)

    order = sorted(range(1, n), key=lambda t: -min(t, n - t))
    for t in order:
        gather_copy(t).start()
    for g in range(1, bands):
        for t in range(n):
            window_copy(g, t).wait_recv()
    for t in order:
        gather_copy(t).wait_recv()

    spot = lane % SLOT
    left = []
    for f in range(cells):
        real, imag = [], []
        for t in range(n):
            x = packed[t, f * ROWS:(f + 1) * ROWS, :]
            real.append(x)
            y = jnp.where(spot < ROWS, -pltpu.roll(x, lanes - ROWS, 1), pltpu.roll(x, ROWS, 1))
            imag.append(jnp.where(spot < PAIR, y, 0.0))
        left += [jnp.concatenate(real, 1), jnp.concatenate(imag, 1)]
    left = jnp.concatenate(left, 0)
    high = left.astype(jnp.bfloat16)
    low = (left - high.astype(jnp.float32)).astype(jnp.bfloat16)
    terms = stack[...].reshape(n * bands * SLOT, window)
    result = dot(high, terms) + dot(low, terms)
    offset = chip * 2 * columns - start

    def cut(c):
        return pltpu.roll(result, window - offset - c * columns, 1)[:, :wide]

    part[...] = cut(1 - core)
    part_copy = pltpu.make_async_remote_copy(
        src_ref=part, dst_ref=part_in, send_sem=one_s.at[2], recv_sem=one_r.at[2],
        device_id=(sibling, band), device_id_type=MESH)
    part_copy.start()
    mine = cut(core)
    part_copy.wait_recv()
    whole = mine + part_in[...]
    for f in range(cells):
        for ri in range(2):
            low_row = (2 * f + ri) * ROWS
            value = whole[low_row:low_row + ROWS] * masks[f]
            out[f, ri] = value[:width, :columns]

    for s in range(1, half + 1):
        for h in range(2):
            for side in (True, False):
                if has(side, s, h):
                    ring_copy(side, s, h).wait_send()
    for g in range(1, bands):
        for t in range(n):
            window_copy(g, t).wait_send()
    for t in order:
        gather_copy(t).wait_send()
    acc_copy.wait_send()
    part_copy.wait_send()


def solution(mesh):
    nk, bands = mesh.shape["ka"], mesh.shape["band"]
    n = nk // 2

    def shards(coefficients, class_weight, diff_class, frag_cells, block_pattern):
        occupied, functions = coefficients.shape[2:]
        width = occupied // bands
        cells, blocks = block_pattern.shape
        padded = (functions + LANES - 1) // LANES * LANES
        columns = functions // nk
        window = (2 * columns + 2 * LANES - 2) // LANES * LANES
        wide = (columns + LANES - 1) // LANES * LANES
        lanes = 2 * bands * STRIDE
        rows = 2 * cells * ROWS
        vmem, smem = pl.BlockSpec(memory_space=pltpu.VMEM), pl.BlockSpec(memory_space=pltpu.SMEM)
        bf16, f32 = jnp.bfloat16, jnp.float32
        dma = pltpu.SemaphoreType.DMA
        return pl.pallas_call(
            functools.partial(kernel, nk, bands, width, occupied, functions, blocks, cells),
            out_shape=jax.ShapeDtypeStruct((cells, 2, width, columns), f32),
            in_specs=[vmem, smem, smem, smem, smem],
            out_specs=vmem,
            scratch_shapes=[
                pltpu.VMEM((2, 2, bands * STRIDE, padded), bf16),
                pltpu.VMEM((n, PAIR, padded), bf16),
                pltpu.VMEM((n, bands, SLOT, window), bf16),
                pltpu.VMEM((rows, lanes), f32),
                pltpu.VMEM((rows, lanes), f32),
                pltpu.VMEM((n, cells * ROWS, lanes), f32),
                pltpu.VMEM((rows, wide), f32),
                pltpu.VMEM((rows, wide), f32),
                dma((n // 2, 2)), dma((n // 2, 2)), dma((n // 2, 2)), dma((n // 2, 2)),
                dma((bands - 1, n)), dma((bands - 1, n)),
                dma((n - 1,)), dma((n - 1,)), dma((3,)), dma((3,)),
            ],
            compiler_params=pltpu.CompilerParams(
                collective_id=0, has_side_effects=True, vmem_limit_bytes=52 * 2**20),
            cost_estimate=pl.CostEstimate(
                flops=2 * n * PAIR * 2 * lanes * padded, bytes_accessed=4 * n * PAIR * padded, transcendentals=0),
            name="exchange",
        )(coefficients, class_weight, diff_class, frag_cells, block_pattern)

    placed = (P("ka", None, None, None), P(), P(), P(), P())
    return jax.shard_map(
        shards, mesh=mesh, in_specs=placed, out_specs=P(None, None, "band", "ka"), check_vma=False)
```

time: 220 us -> 41.5 us (0.19)
  waiting for transfers between devices: 187 us -> 0 us
  Pallas kernels: 0 us -> 36.9 us
  between operations: 14.5 us -> 0.01 us
  other arithmetic: 6.64 us -> 0 us
  local copies, waits for them, and re-layouts: 8.09 us -> 4.36 us
  matrix products: 2.78 us -> 0 us
    unnamed x5 -> x0, waiting for transfers between devices: 141 us -> none
    all_gather x1 -> x0, waiting for transfers between devices: 46.6 us -> none  [shards(): piece = lax.all_gather(my_group[None], 'ka', axis=0, tiled=True)]
    pallas_call x0 -> x1, Pallas kernels: none -> 36.9 us  [shards(): pl.pallas_call(functools.partial(kernel, nk, bands, width, occupied, func...]
    dot_general x4 -> x0, matrix products: 2.78 us -> none  [the longest x1 0.96 us: shards(): jnp.einsum('qia,ja->qij', blocks, own_flat, preferred_element_type=jnp.fl...]
    another operation x1 -> x0, other arithmetic: 2.56 us -> none  [shards(): jnp.stack([cosines * w_real - sines * w_imag, sines * w_real + cosines *...]
    unnamed x12 -> x10, local copies, waits for them, and re-layouts: 5.08 us -> 3.68 us
  transfers between devices with their start and end apart: 3 -> 0, of which waited for: 3 -> 0; matrix products, arithmetic and copies ran while one was open for 2% -> 0% of each run, Pallas kernels for 0% -> 0%
where the time goes in v1:
time: 41.5 us; the launch traced here: 41.3 us
  Pallas kernels  36.9 us (89%)
  local copies, waits for them, and re-layouts  4.36 us (11%)
    pallas_call x1, Pallas kernels, shards(): pl.pallas_call(functools.partial(kernel, nk, bands, width, occupied, func...  36.9 us
    unnamed x10, local copies, waits for them, and re-layouts  3.68 us

profile of v1, /device:TPU:0, one launch (start us, length us, event | category | flops | bytes accessed | tf_op | source)
XLA Modules:
  0.0 41.3 jit_solution(17241124610125563538)
XLA Ops:
  0.0 0.0 copy-start
  0.0 1.0 %copy-done = bf16[1,2,40,2400]{3,2,1,0:T(8,128)(2,1)S(1)} copy-done((bf16[1,2,40,2400]{3,2,1,0:T(8,128)(2,1)S(1)}, bf16[1,2,40,2400]{3,2,1,0:T(8,128)(2,1)}, u32[]{:S(2)}) %copy-start) | copy-done | bytes 384024
  1.0 0.0 copy-start.1
  1.0 0.7 %copy-done.1 = s32[16,16]{1,0:T(8,128)S(1)} copy-done((s32[16,16]{1,0:T(8,128)S(1)}, s32[16,16]{1,0:T(8,128)}, u32[]{:S(2)}) %copy-start.1) | copy-done | bytes 1048
  1.7 0.0 copy-start.2
  1.7 0.7 %copy-done.2 = s32[2,30]{1,0:T(2,128)S(1)} copy-done((s32[2,30]{1,0:T(2,128)S(1)}, s32[2,30]{1,0:T(2,128)}, u32[]{:S(2)}) %copy-start.2) | copy-done | bytes 264
  2.4 0.0 copy-start.3
  2.4 0.7 %copy-done.3 = f32[16]{0:T(128)S(1)} copy-done((f32[16]{0:T(128)S(1)}, f32[16]{0:T(128)}, u32[]{:S(2)}) %copy-start.3) | copy-done | bytes 88
  3.0 0.0 copy-start.4
  3.0 0.7 %copy-done.4 = s32[2]{0:T(128)S(1)} copy-done((s32[2]{0:T(128)S(1)}, s32[2]{0:T(128)}, u32[]{:S(2)}) %copy-start.4) | copy-done | bytes 32
  3.7 36.9 %exchange.1 = f32[2,2,20,150]{3,2,1,0:T(8,128)S(1)} custom-call(bf16[1,2,40,2400]{3,2,1,0:T(8,128)(2,1)S(1)} %copy-done, f32[16]{0:T(128)S(1)} %copy-done.3, s32[16,16]{1,0:T(8,128)S(1)} %copy-done.1, s32[2]{0:T(128)S(1)} %copy-done.4, s32[2,30]{1,0:T(2,128)S(1)} %copy-done.2), custom_call_target="tpu_custom_call" | custom-call | flops 478150656 | bytes 3735552 | tf_op jit(solution)/shard_map/exchange/pallas_call | solution.py:282
  40.6 0.7 %copy.6 = f32[2,2,20,150]{3,1,2,0:T(2,128)} copy(f32[2,2,20,150]{3,2,1,0:T(8,128)S(1)} %exchange.1) | data formatting | bytes 96000 | tf_op jit(solution)/shard_map/exchange/pallas_call | solution.py:282
Async XLA Ops:
  0.0 1.0 %copy-start = (bf16[1,2,40,2400]{3,2,1,0:T(8,128)(2,1)S(1)}, bf16[1,2,40,2400]{3,2,1,0:T(8,128)(2,1)}, u32[]{:S(2)}) copy-start(bf16[1,2,40,2400]{3,2,1,0:T(8,128)(2,1)} %own.1) | copy-start | bytes 1152004
  1.0 0.7 %copy-start.1 = (s32[16,16]{1,0:T(8,128)S(1)}, s32[16,16]{1,0:T(8,128)}, u32[]{:S(2)}) copy-start(s32[16,16]{1,0:T(8,128)} %classes.1) | copy-start | bytes 3076
  1.7 0.7 %copy-start.2 = (s32[2,30]{1,0:T(2,128)S(1)}, s32[2,30]{1,0:T(2,128)}, u32[]{:S(2)}) copy-start(s32[2,30]{1,0:T(2,128)} %pattern.1) | copy-start | bytes 724
  2.4 0.7 %copy-start.3 = (f32[16]{0:T(128)S(1)}, f32[16]{0:T(128)}, u32[]{:S(2)}) copy-start(f32[16]{0:T(128)} %weight.1) | copy-start | bytes 196
  3.0 0.7 %copy-start.4 = (s32[2]{0:T(128)S(1)}, s32[2]{0:T(128)}, u32[]{:S(2)}) copy-start(s32[2]{0:T(128)} %frag.1) | copy-start | bytes 28

commit v2 on v1

v2 whole, which is shorter than its diff:
```python
import functools
import math

import jax
import jax.numpy as jnp
from jax import lax
from jax.experimental import pallas as pl
from jax.experimental.pallas import tpu as pltpu
from jax.sharding import PartitionSpec as P

MESH = pl.DeviceIdType.MESH
LANES = 128
STRIDE = 32


def kernel(nk, bands, width, occupied, functions, blocks, cells,
           own_hbm, weight_hbm, classes_hbm, frag_hbm, pattern_hbm, out,
           own, weight, classes, frag, pattern,
           sel, slots, near, stack, acc, acc_in, packed, part, part_in,
           in_s, right_s, right_r, left_s, left_r, win_s, win_r, gat_s, gat_r, one_s, one_r):
    n = nk // 2
    half = n // 2
    ka, band = lax.axis_index("ka"), lax.axis_index("band")
    chip, core = ka // 2, ka % 2
    padded = slots.shape[2]
    tiles = padded // LANES
    first = (tiles + 1) // 2 * LANES
    chunks = (pl.ds(0, first), pl.ds(first, padded - first))
    window = stack.shape[2]
    columns = functions // nk
    lanes = 2 * bands * STRIDE
    rows = cells * width
    f32, bf16 = jnp.float32, jnp.bfloat16

    operands = (own_hbm, weight_hbm, classes_hbm, frag_hbm, pattern_hbm)
    fetches = [pltpu.make_async_copy(src, dst, in_s.at[i])
               for i, (src, dst) in enumerate(zip(operands, (own, weight, classes, frag, pattern)))]
    for fetch in fetches:
        fetch.start()

    def chip_at(ring):
        return jnp.where(ring < half, 2 * ring, 2 * (n - 1 - ring) + 1)

    row, odd = chip // 2, chip % 2
    ring = jnp.where(odd == 0, row, n - 1 - row)

    def member(offset):
        return 2 * chip_at((ring + offset + n) % n) + core

    sibling = 2 * chip + 1 - core
    barrier = pltpu.get_barrier_semaphore()
    for offset in range(1, n):
        pl.semaphore_signal(barrier, inc=1, device_id=(member(offset), band), device_id_type=MESH)
    pl.semaphore_signal(barrier, inc=1, device_id=(sibling, band), device_id_type=MESH)
    for offset in range(1, bands):
        pl.semaphore_signal(barrier, inc=1, device_id=(ka, (band + offset) % bands), device_id_type=MESH)

    def dot(a, b):
        return jnp.dot(a, b, preferred_element_type=f32)

    def iotas(shape):
        return (lax.broadcasted_iota(jnp.int32, shape, 0), lax.broadcasted_iota(jnp.int32, shape, 1))

    slots[0, :, padded - LANES:] = jnp.zeros((2 * width, LANES), bf16)
    r, c = iotas((2 * width, occupied))
    c = c - band * width
    pick_re = jnp.where((c >= 0) & (c < width) & (c == r), 1.0, 0.0).astype(bf16)
    pick_im = jnp.where((c >= 0) & (c < width) & (c == r - width), 1.0, 0.0).astype(bf16)
    fetches[0].wait()
    re, im = own[0, 0], own[0, 1]
    slots[0, :, :functions] = (dot(pick_re, re) + dot(pick_im, im)).astype(bf16)

    pl.semaphore_wait(barrier, n - 1 + 1 + bands - 1)

    def ring_copy(to_right, s, h):
        if to_right:
            src, dst, ss, rs, to = s - 1, s, right_s, right_r, member(1)
        else:
            src, dst, ss, rs, to = (n - s + 1) % n, n - s, left_s, left_r, member(-1)
        return pltpu.make_async_remote_copy(
            src_ref=slots.at[src, :, chunks[h]], dst_ref=slots.at[dst, :, chunks[h]],
            send_sem=ss.at[s - 1, h], recv_sem=rs.at[s - 1, h],
            device_id=(to, band), device_id_type=MESH)

    def has(to_right, s, h):
        return s < half or (s == half and h == (0 if to_right else 1))

    start = pl.multiple_of(jnp.minimum(chip * 2 * columns // LANES, tiles - window // LANES) * LANES, LANES)

    def window_copy(g, t):
        return pltpu.make_async_remote_copy(
            src_ref=slots.at[t, :, pl.ds(start, window)], dst_ref=near.at[g - 1, t],
            send_sem=win_s.at[g - 1, t], recv_sem=win_r.at[g - 1, t],
            device_id=(ka, (band + g) % bands), device_id_type=MESH)

    def spread(t):
        for g in range(1, bands):
            window_copy(g, t).start()

    for h in range(2):
        for side in (True, False):
            if has(side, 1, h):
                ring_copy(side, 1, h).start()
    spread(0)

    r, c = iotas((occupied, lanes))
    hits = [jnp.zeros(r.shape, f32), jnp.zeros(r.shape, f32)]
    for ri in range(2):
        for g in range(bands):
            low = (ri * bands + g) * STRIDE
            inside = (c >= low) & (c < low + width)
            hits[ri] = jnp.where(inside & (r - ((band - g + bands) % bands) * width == c - low), 1.0, hits[ri])
    mine = pl.ds(pl.multiple_of(core * lanes, LANES), lanes)
    sel[padded - LANES:, mine] = jnp.zeros((LANES, lanes), bf16)

    def turned(value, hit):
        return lax.dot_general(value, hit.astype(bf16), (((0,), (0,)), ((), ())), preferred_element_type=f32)

    sel[:functions, mine] = (turned(re, hits[0]) + turned(im, hits[1])).astype(bf16)
    sel_copy = pltpu.make_async_remote_copy(
        src_ref=sel.at[:, mine], dst_ref=sel.at[:, mine], send_sem=one_s.at[0], recv_sem=one_r.at[0],
        device_id=(sibling, band), device_id_type=MESH)
    sel_copy.start()
    for fetch in fetches[1:]:
        fetch.wait()

    at = lax.broadcasted_iota(jnp.int32, (n, 2 * lanes), 0)
    where = ring - at
    where = jnp.where(where < 0, where + n, where)
    kpoint = (2 * chip_at(where) + core).astype(f32)
    lane = lax.broadcasted_iota(jnp.int32, (n, 2 * lanes), 1)
    sign = jnp.where(lane % lanes < lanes // 2, 1.0, -1.0)
    cosines, sines = [], []
    for f in range(cells):
        turns = kpoint * (frag[f].astype(f32) / nk)
        angle = 2.0 * math.pi * (turns - jnp.floor(turns))
        cosines.append(jnp.cos(angle) / nk)
        sines.append(sign * jnp.sin(angle) / nk)
    wide = (columns + LANES - 1) // LANES * LANES
    column = lax.broadcasted_iota(jnp.int32, (width, wide), 1) + ka * columns
    block = functions // blocks
    masks = []
    for f in range(cells):
        mask = jnp.zeros((width, wide), f32)
        for i in range(blocks):
            keep = (column >= i * block) & (column < (i + 1) * block)
            mask = jnp.where(keep, pattern[f, i].astype(f32), mask)
        masks.append(mask)

    def swap(x):
        return pltpu.roll(x, lanes // 2, 1)

    def swap_both(x):
        return jnp.concatenate([swap(x[:, :lanes]), swap(x[:, lanes:])], 1)

    own_lane = lax.broadcasted_iota(jnp.int32, (width, 2 * lanes), 1)
    signs = jnp.where(own_lane % lanes < lanes // 2, 1.0, -1.0)

    def overlap(t):
        k = member(-t)
        product = dot(slots[t], sel[...])
        value = product[:width] + signs * swap_both(product[width:])
        scale = jnp.where(own_lane < lanes, weight[classes[k, 2 * chip]], weight[classes[k, 2 * chip + 1]])
        value = (scale / functions * value).astype(bf16).astype(f32)
        other = swap_both(value)
        terms = jnp.concatenate(
            [cosines[f][t:t + 1] * value + sines[f][t:t + 1] * other for f in range(cells)], 0)
        if t == 0:
            acc[...] = terms
        else:
            acc[...] += terms

    r, c = iotas((lanes, 2 * width))
    placers = []
    for g in range(bands):
        a, b = g * STRIDE, (bands + g) * STRIDE
        hit = ((c < width) & (r == a + c)) | ((c >= width) & (r == b + c - width))
        placers.append(jnp.where(hit, 1.0, 0.0).astype(bf16))

    def place(t):
        value = dot(placers[0], slots[t, :, pl.ds(start, window)])
        for g in range(1, bands):
            window_copy(g, t).wait_recv()
            value = value + dot(placers[g], near[g - 1, t])
        stack[t] = value.astype(bf16)

    sel_copy.wait()
    for s in range(1, half + 1):
        before = [s - 1] if s == 1 else [s - 1, n - s + 1]
        for h in range(2):
            for side in (True, False):
                if has(side, s, h):
                    ring_copy(side, s, h).wait_recv()
                    if has(side, s + 1, h):
                        ring_copy(side, s + 1, h).start()
            if h == 0:
                overlap(before[0])
        spread(s)
        if s < half:
            spread(n - s)
        for t in before[1:]:
            overlap(t)
        if s < half:
            for t in before:
                place(t)
    overlap(half)

    acc_copy = pltpu.make_async_remote_copy(
        src_ref=acc, dst_ref=acc_in, send_sem=one_s.at[1], recv_sem=one_r.at[1],
        device_id=(sibling, band), device_id_type=MESH)
    acc_copy.start()
    acc_copy.wait_recv()
    packed[0] = acc[:, mine] + acc_in[:, mine]

    def gather_copy(t):
        return pltpu.make_async_remote_copy(
            src_ref=packed.at[0], dst_ref=packed.at[t], send_sem=gat_s.at[t - 1], recv_sem=gat_r.at[t - 1],
            device_id=(member(t), band), device_id_type=MESH)

    order = sorted(range(1, n), key=lambda t: -min(t, n - t))
    for t in order:
        gather_copy(t).start()
    for t in (half - 1, half + 1, half):
        place(t)
    for t in order:
        gather_copy(t).wait_recv()

    rotated = lax.broadcasted_iota(jnp.int32, (rows, lanes), 1)
    flip = jnp.where(rotated < lanes // 2, -1.0, 1.0)
    real = [packed[t] for t in range(n)]
    left = jnp.concatenate(
        [jnp.concatenate(real, 1), jnp.concatenate([flip * swap(x) for x in real], 1)], 0)
    high = left.astype(bf16)
    low = (left - high.astype(f32)).astype(bf16)
    terms = stack[...].reshape(n * lanes, window)
    result = dot(high, terms) + dot(low, terms)
    offset = chip * 2 * columns - start

    def cut(c):
        return pltpu.roll(result, window - offset - c * columns, 1)[:, :wide]

    part[...] = cut(1 - core)
    part_copy = pltpu.make_async_remote_copy(
        src_ref=part, dst_ref=part_in, send_sem=one_s.at[2], recv_sem=one_r.at[2],
        device_id=(sibling, band), device_id_type=MESH)
    part_copy.start()
    kept = cut(core)
    part_copy.wait_recv()
    whole = kept + part_in[...]
    for ri in range(2):
        for f in range(cells):
            spot = (ri * cells + f) * width
            out[f, ri] = (whole[spot:spot + width] * masks[f])[:, :columns]

    for s in range(1, half + 1):
        for h in range(2):
            for side in (True, False):
                if has(side, s, h):
                    ring_copy(side, s, h).wait_send()
    for g in range(1, bands):
        for t in range(n):
            window_copy(g, t).wait_send()
    for t in order:
        gather_copy(t).wait_send()
    acc_copy.wait_send()
    part_copy.wait_send()


def solution(mesh):
    nk, bands = mesh.shape["ka"], mesh.shape["band"]
    n = nk // 2

    def shards(coefficients, class_weight, diff_class, frag_cells, block_pattern):
        occupied, functions = coefficients.shape[2:]
        width = occupied // bands
        cells, blocks = block_pattern.shape
        padded = (functions + LANES - 1) // LANES * LANES
        columns = functions // nk
        window = (2 * columns + 2 * LANES - 2) // LANES * LANES
        wide = (columns + LANES - 1) // LANES * LANES
        lanes = 2 * bands * STRIDE
        rows = cells * width
        hbm = pl.BlockSpec(memory_space=pl.ANY)
        bf16, f32 = jnp.bfloat16, jnp.float32
        dma = pltpu.SemaphoreType.DMA
        operands = (coefficients, class_weight, diff_class, frag_cells, block_pattern)
        return pl.pallas_call(
            functools.partial(kernel, nk, bands, width, occupied, functions, blocks, cells),
            out_shape=jax.ShapeDtypeStruct((cells, 2, width, columns), f32),
            in_specs=[hbm] * 5,
            out_specs=pl.BlockSpec(memory_space=pltpu.VMEM),
            scratch_shapes=[
                pltpu.VMEM(coefficients.shape, bf16),
                *[pltpu.SMEM(x.shape, x.dtype) for x in operands[1:]],
                pltpu.VMEM((padded, 2 * lanes), bf16),
                pltpu.VMEM((n, 2 * width, padded), bf16),
                pltpu.VMEM((bands - 1, n, 2 * width, window), bf16),
                pltpu.VMEM((n, lanes, window), bf16),
                pltpu.VMEM((rows, 2 * lanes), f32),
                pltpu.VMEM((rows, 2 * lanes), f32),
                pltpu.VMEM((n, rows, lanes), f32),
                pltpu.VMEM((2 * rows, wide), f32),
                pltpu.VMEM((2 * rows, wide), f32),
                dma((5,)),
                dma((n // 2, 2)), dma((n // 2, 2)), dma((n // 2, 2)), dma((n // 2, 2)),
                dma((bands - 1, n)), dma((bands - 1, n)),
                dma((n - 1,)), dma((n - 1,)), dma((3,)), dma((3,)),
            ],
            compiler_params=pltpu.CompilerParams(
                collective_id=0, has_side_effects=True, vmem_limit_bytes=52 * 2**20),
            cost_estimate=pl.CostEstimate(
                flops=8 * n * width * lanes * padded, bytes_accessed=8 * n * width * padded, transcendentals=0),
            name="exchange",
        )(*operands)

    placed = (P("ka", None, None, None), P(), P(), P(), P())
    return jax.shard_map(
        shards, mesh=mesh, in_specs=placed, out_specs=P(None, None, "band", "ka"), check_vma=False)
```

time: 41.5 us -> 38.7 us (0.933)
  Pallas kernels: 36.9 us -> 34.1 us
    pallas_call x1, Pallas kernels: 36.9 us -> 34.1 us  [shards(): pl.pallas_call(functools.partial(kernel, nk, bands, width, occupied, func...]
where the time goes in v2:
time: 38.7 us; the launch traced here: 38.5 us
  Pallas kernels  34.1 us (88%)
  local copies, waits for them, and re-layouts  4.36 us (11%)
    pallas_call x1, Pallas kernels, shards(): pl.pallas_call(functools.partial(kernel, nk, bands, width, occupied, func...  34.1 us
    unnamed x10, local copies, waits for them, and re-layouts  3.68 us

profile of v2, /device:TPU:0, one launch (start us, length us, event | category | flops | bytes accessed | tf_op | source)
XLA Modules:
  0.0 38.5 jit_solution(15291700316105206563)
XLA Ops:
  0.0 0.0 copy-start
  0.0 1.0 %copy-done = bf16[1,2,40,2400]{3,2,1,0:T(8,128)(2,1)S(1)} copy-done((bf16[1,2,40,2400]{3,2,1,0:T(8,128)(2,1)S(1)}, bf16[1,2,40,2400]{3,2,1,0:T(8,128)(2,1)}, u32[]{:S(2)}) %copy-start) | copy-done | bytes 384024
  1.0 0.0 copy-start.1
  1.0 0.7 %copy-done.1 = s32[16,16]{1,0:T(8,128)S(1)} copy-done((s32[16,16]{1,0:T(8,128)S(1)}, s32[16,16]{1,0:T(8,128)}, u32[]{:S(2)}) %copy-start.1) | copy-done | bytes 1048
  1.7 0.0 copy-start.2
  1.7 0.7 %copy-done.2 = s32[2,30]{1,0:T(2,128)S(1)} copy-done((s32[2,30]{1,0:T(2,128)S(1)}, s32[2,30]{1,0:T(2,128)}, u32[]{:S(2)}) %copy-start.2) | copy-done | bytes 264
  2.4 0.0 copy-start.3
  2.4 0.7 %copy-done.3 = f32[16]{0:T(128)S(1)} copy-done((f32[16]{0:T(128)S(1)}, f32[16]{0:T(128)}, u32[]{:S(2)}) %copy-start.3) | copy-done | bytes 88
  3.0 0.0 copy-start.4
  3.0 0.7 %copy-done.4 = s32[2]{0:T(128)S(1)} copy-done((s32[2]{0:T(128)S(1)}, s32[2]{0:T(128)}, u32[]{:S(2)}) %copy-start.4) | copy-done | bytes 32
  3.7 34.1 %exchange.1 = f32[2,2,20,150]{3,2,1,0:T(8,128)S(1)} custom-call(bf16[1,2,40,2400]{3,2,1,0:T(8,128)(2,1)S(1)} %copy-done, f32[16]{0:T(128)S(1)} %copy-done.3, s32[16,16]{1,0:T(8,128)S(1)} %copy-done.1, s32[2]{0:T(128)S(1)} %copy-done.4, s32[2,30]{1,0:T(2,128)S(1)} %copy-done.2), custom_call_target="tpu_custom_call" | custom-call | flops 398458880 | bytes 3112960 | tf_op jit(solution)/shard_map/exchange/pallas_call | solution.py:287
  37.8 0.7 %copy.6 = f32[2,2,20,150]{3,1,2,0:T(2,128)} copy(f32[2,2,20,150]{3,2,1,0:T(8,128)S(1)} %exchange.1) | data formatting | bytes 96000 | tf_op jit(solution)/shard_map/exchange/pallas_call | solution.py:287
Async XLA Ops:
  0.0 1.0 %copy-start = (bf16[1,2,40,2400]{3,2,1,0:T(8,128)(2,1)S(1)}, bf16[1,2,40,2400]{3,2,1,0:T(8,128)(2,1)}, u32[]{:S(2)}) copy-start(bf16[1,2,40,2400]{3,2,1,0:T(8,128)(2,1)} %own_hbm.1) | copy-start | bytes 1152004
  1.0 0.7 %copy-start.1 = (s32[16,16]{1,0:T(8,128)S(1)}, s32[16,16]{1,0:T(8,128)}, u32[]{:S(2)}) copy-start(s32[16,16]{1,0:T(8,128)} %classes_hbm.1) | copy-start | bytes 3076
  1.7 0.7 %copy-start.2 = (s32[2,30]{1,0:T(2,128)S(1)}, s32[2,30]{1,0:T(2,128)}, u32[]{:S(2)}) copy-start(s32[2,30]{1,0:T(2,128)} %pattern_hbm.1) | copy-start | bytes 724
  2.4 0.7 %copy-start.3 = (f32[16]{0:T(128)S(1)}, f32[16]{0:T(128)}, u32[]{:S(2)}) copy-start(f32[16]{0:T(128)} %weight_hbm.1) | copy-start | bytes 196
  3.0 0.7 %copy-start.4 = (s32[2]{0:T(128)S(1)}, s32[2]{0:T(128)}, u32[]{:S(2)}) copy-start(s32[2]{0:T(128)} %frag_hbm.1) | copy-start | bytes 28

commit v3 on v2

--- a/solution.py
+++ b/solution.py
@@ -16,7 +16,7 @@
 def kernel(nk, bands, width, occupied, functions, blocks, cells,
            own_hbm, weight_hbm, classes_hbm, frag_hbm, pattern_hbm, out,
            own, weight, classes, frag, pattern,
-           sel, slots, near, stack, acc, acc_in, packed, part, part_in,
+           sel, slots, near, stack, turn, acc, acc_in, packed, part, part_in,
            in_s, right_s, right_r, left_s, left_r, win_s, win_r, gat_s, gat_r, one_s, one_r):
     n = nk // 2
     half = n // 2
@@ -44,8 +44,17 @@
     row, odd = chip // 2, chip % 2
     ring = jnp.where(odd == 0, row, n - 1 - row)
 
+    def wrap(x):
+        x = jnp.where(x >= n, x - n, x)
+        return jnp.where(x < 0, x + n, x)
+
+    members = [2 * chip_at(wrap(ring + offset)) + core for offset in range(n)]
+
     def member(offset):
-        return 2 * chip_at((ring + offset + n) % n) + core
+        return members[offset % n]
+
+    def place_of(t):
+        return 2 * t - 1 if 0 < t <= half else 2 * ((n - t) % n)
 
     sibling = 2 * chip + 1 - core
     barrier = pltpu.get_barrier_semaphore()
@@ -74,16 +83,17 @@
 
     def ring_copy(to_right, s, h):
         if to_right:
-            src, dst, ss, rs, to = s - 1, s, right_s, right_r, member(1)
+            src, dst, ss, rs, to = jnp.maximum(2 * s - 3, 0), 2 * s - 1, right_s, right_r, member(1)
         else:
-            src, dst, ss, rs, to = (n - s + 1) % n, n - s, left_s, left_r, member(-1)
+            dst = jnp.where(s == half, n - 1, 2 * s)
+            src, ss, rs, to = 2 * s - 2, left_s, left_r, member(-1)
         return pltpu.make_async_remote_copy(
             src_ref=slots.at[src, :, chunks[h]], dst_ref=slots.at[dst, :, chunks[h]],
             send_sem=ss.at[s - 1, h], recv_sem=rs.at[s - 1, h],
             device_id=(to, band), device_id_type=MESH)
 
-    def has(to_right, s, h):
-        return s < half or (s == half and h == (0 if to_right else 1))
+    def steps(to_right, h):
+        return half if h == (0 if to_right else 1) else half - 1
 
     start = pl.multiple_of(jnp.minimum(chip * 2 * columns // LANES, tiles - window // LANES) * LANES, LANES)
 
@@ -99,8 +109,7 @@
 
     for h in range(2):
         for side in (True, False):
-            if has(side, 1, h):
-                ring_copy(side, 1, h).start()
+            ring_copy(side, 1, h).start()
     spread(0)
 
     r, c = iotas((occupied, lanes))
@@ -125,17 +134,15 @@
         fetch.wait()
 
     at = lax.broadcasted_iota(jnp.int32, (n, 2 * lanes), 0)
-    where = ring - at
-    where = jnp.where(where < 0, where + n, where)
+    where = wrap(jnp.where(at % 2 == 0, ring + at // 2, ring - at // 2 - 1))
     kpoint = (2 * chip_at(where) + core).astype(f32)
     lane = lax.broadcasted_iota(jnp.int32, (n, 2 * lanes), 1)
     sign = jnp.where(lane % lanes < lanes // 2, 1.0, -1.0)
-    cosines, sines = [], []
     for f in range(cells):
         turns = kpoint * (frag[f].astype(f32) / nk)
         angle = 2.0 * math.pi * (turns - jnp.floor(turns))
-        cosines.append(jnp.cos(angle) / nk)
-        sines.append(sign * jnp.sin(angle) / nk)
+        turn[f] = jnp.cos(angle) / nk
+        turn[cells + f] = sign * jnp.sin(angle) / nk
     wide = (columns + LANES - 1) // LANES * LANES
     column = lax.broadcasted_iota(jnp.int32, (width, wide), 1) + ka * columns
     block = functions // blocks
@@ -156,19 +163,19 @@
     own_lane = lax.broadcasted_iota(jnp.int32, (width, 2 * lanes), 1)
     signs = jnp.where(own_lane % lanes < lanes // 2, 1.0, -1.0)
 
-    def overlap(t):
-        k = member(-t)
-        product = dot(slots[t], sel[...])
-        value = product[:width] + signs * swap_both(product[width:])
-        scale = jnp.where(own_lane < lanes, weight[classes[k, 2 * chip]], weight[classes[k, 2 * chip + 1]])
-        value = (scale / functions * value).astype(bf16).astype(f32)
-        other = swap_both(value)
-        terms = jnp.concatenate(
-            [cosines[f][t:t + 1] * value + sines[f][t:t + 1] * other for f in range(cells)], 0)
-        if t == 0:
-            acc[...] = terms
-        else:
-            acc[...] += terms
+    def overlap(i):
+        both = slots[pl.ds(2 * i, 2)].reshape(4 * width, padded)
+        product = dot(both, sel[...])
+        for side in range(2):
+            low = 2 * width * side
+            k = 2 * chip_at(wrap(ring - i - 1 if side else ring + i)) + core
+            value = product[low:low + width] + signs * swap_both(product[low + width:low + 2 * width])
+            scale = jnp.where(own_lane < lanes, weight[classes[k, 2 * chip]], weight[classes[k, 2 * chip + 1]])
+            value = (scale / functions * value).astype(bf16).astype(f32)
+            other = swap_both(value)
+            at = pl.ds(2 * i + side, 1)
+            acc[...] += jnp.concatenate(
+                [turn[f, at, :] * value + turn[cells + f, at, :] * other for f in range(cells)], 0)
 
     r, c = iotas((lanes, 2 * width))
     placers = []
@@ -184,26 +191,30 @@
             value = value + dot(placers[g], near[g - 1, t])
         stack[t] = value.astype(bf16)
 
+    acc[...] = jnp.zeros((rows, 2 * lanes), f32)
     sel_copy.wait()
-    for s in range(1, half + 1):
-        before = [s - 1] if s == 1 else [s - 1, n - s + 1]
+
+    @pl.loop(0, half)
+    def _(i):
+        s = i + 1
         for h in range(2):
             for side in (True, False):
-                if has(side, s, h):
+                last = steps(side, h)
+
+                @pl.when(s <= last)
+                def _():
                     ring_copy(side, s, h).wait_recv()
-                    if has(side, s + 1, h):
-                        ring_copy(side, s + 1, h).start()
-            if h == 0:
-                overlap(before[0])
-        spread(s)
-        if s < half:
-            spread(n - s)
-        for t in before[1:]:
-            overlap(t)
-        if s < half:
-            for t in before:
-                place(t)
-    overlap(half)
+
+                @pl.when(s < last)
+                def _():
+                    ring_copy(side, s + 1, h).start()
+        spread(2 * s - 1)
+
+        @pl.when(s < half)
+        def _():
+            spread(2 * s)
+
+        overlap(i)
 
     acc_copy = pltpu.make_async_remote_copy(
         src_ref=acc, dst_ref=acc_in, send_sem=one_s.at[1], recv_sem=one_r.at[1],
@@ -214,14 +225,13 @@
 
     def gather_copy(t):
         return pltpu.make_async_remote_copy(
-            src_ref=packed.at[0], dst_ref=packed.at[t], send_sem=gat_s.at[t - 1], recv_sem=gat_r.at[t - 1],
+            src_ref=packed.at[0], dst_ref=packed.at[place_of(t)], send_sem=gat_s.at[t - 1], recv_sem=gat_r.at[t - 1],
             device_id=(member(t), band), device_id_type=MESH)
 
     order = sorted(range(1, n), key=lambda t: -min(t, n - t))
     for t in order:
         gather_copy(t).start()
-    for t in (half - 1, half + 1, half):
-        place(t)
+    pl.loop(0, n)(place)
     for t in order:
         gather_copy(t).wait_recv()
 
@@ -233,7 +243,8 @@
     high = left.astype(bf16)
     low = (left - high.astype(f32)).astype(bf16)
     terms = stack[...].reshape(n * lanes, window)
-    result = dot(high, terms) + dot(low, terms)
+    result = dot(jnp.concatenate([high, low], 0), terms)
+    result = result[:2 * rows] + result[2 * rows:]
     offset = chip * 2 * columns - start
 
     def cut(c):
@@ -252,14 +263,19 @@
             spot = (ri * cells + f) * width
             out[f, ri] = (whole[spot:spot + width] * masks[f])[:, :columns]
 
-    for s in range(1, half + 1):
+    @pl.loop(1, half + 1)
+    def _(s):
         for h in range(2):
             for side in (True, False):
-                if has(side, s, h):
+                @pl.when(s <= steps(side, h))
+                def _():
                     ring_copy(side, s, h).wait_send()
-    for g in range(1, bands):
-        for t in range(n):
+
+    @pl.loop(0, n)
+    def _(t):
+        for g in range(1, bands):
             window_copy(g, t).wait_send()
+
     for t in order:
         gather_copy(t).wait_send()
     acc_copy.wait_send()
@@ -280,7 +296,7 @@
         wide = (columns + LANES - 1) // LANES * LANES
         lanes = 2 * bands * STRIDE
         rows = cells * width
-        hbm = pl.BlockSpec(memory_space=pl.ANY)
+        hbm = pl.BlockSpec(memory_space=pltpu.HBM)
         bf16, f32 = jnp.bfloat16, jnp.float32
         dma = pltpu.SemaphoreType.DMA
         operands = (coefficients, class_weight, diff_class, frag_cells, block_pattern)
@@ -296,6 +312,7 @@
                 pltpu.VMEM((n, 2 * width, padded), bf16),
                 pltpu.VMEM((bands - 1, n, 2 * width, window), bf16),
                 pltpu.VMEM((n, lanes, window), bf16),
+                pltpu.VMEM((2 * cells, n, 2 * lanes), f32),
                 pltpu.VMEM((rows, 2 * lanes), f32),
                 pltpu.VMEM((rows, 2 * lanes), f32),
                 pltpu.VMEM((n, rows, lanes), f32),
@@ -307,7 +324,7 @@
                 dma((n - 1,)), dma((n - 1,)), dma((3,)), dma((3,)),
             ],
             compiler_params=pltpu.CompilerParams(
-                collective_id=0, has_side_effects=True, vmem_limit_bytes=52 * 2**20),
+                collective_id=0, has_side_effects=True, vmem_limit_bytes=63 * 2**20),
             cost_estimate=pl.CostEstimate(
                 flops=8 * n * width * lanes * padded, bytes_accessed=8 * n * width * padded, transcendentals=0),
             name="exchange",

time: 38.7 us -> 35.3 us (0.912)
  local copies, waits for them, and re-layouts: 4.36 us -> 1.57 us
  Pallas kernels: 34.1 us -> 33.5 us
    unnamed x10 -> x0, local copies, waits for them, and re-layouts: 3.68 us -> none
    pallas_call x1, local copies, waits for them, and re-layouts: 0.68 us -> 1.57 us  [shards(): pl.pallas_call(functools.partial(kernel, nk, bands, width, occupied, func...]
    pallas_call x1, Pallas kernels: 34.1 us -> 33.5 us  [shards(): pl.pallas_call(functools.partial(kernel, nk, bands, width, occupied, func...]
where the time goes in v3:
time: 35.3 us; the launch traced here: 35.1 us
  Pallas kernels  33.5 us (95%)
  local copies, waits for them, and re-layouts  1.57 us (4%)
    pallas_call x1, Pallas kernels, shards(): pl.pallas_call(functools.partial(kernel, nk, bands, width, occupied, func...  33.5 us
    pallas_call x1, local copies, waits for them, and re-layouts, shards(): pl.pallas_call(functools.partial(kernel, nk, bands, width, occupied, func...  1.57 us

profile of v3, /device:TPU:0, one launch (start us, length us, event | category | flops | bytes accessed | tf_op | source)
XLA Modules:
  0.0 35.1 jit_solution(3997152136633074041)
XLA Ops:
  0.0 33.5 %exchange.1 = f32[2,2,20,150]{3,2,1,0:T(8,128)} custom-call(bf16[1,2,40,2400]{3,2,1,0:T(8,128)(2,1)} %own_hbm.1, f32[16]{0:T(128)} %weight_hbm.1, s32[16,16]{1,0:T(8,128)} %classes_hbm.1, s32[2]{0:T(128)} %frag_hbm.1, s32[2,30]{1,0:T(2,128)} %pattern_hbm.1), custom_call_target="tpu_custom_call" | custom-call | flops 398458880 | bytes 3112960 | tf_op jit(solution)/shard_map/exchange/pallas_call | solution.py:303
  33.5 1.6 %copy.6 = f32[2,2,20,150]{3,1,2,0:T(2,128)} copy(f32[2,2,20,150]{3,2,1,0:T(8,128)} %exchange.1) | data formatting | bytes 96000 | tf_op jit(solution)/shard_map/exchange/pallas_call | solution.py:303

commit v4 on v3

--- a/solution.py
+++ b/solution.py
@@ -26,7 +26,7 @@
     tiles = padded // LANES
     first = (tiles + 1) // 2 * LANES
     chunks = (pl.ds(0, first), pl.ds(first, padded - first))
-    window = stack.shape[2]
+    window, wide = near.shape[3], stack.shape[3]
     columns = functions // nk
     lanes = 2 * bands * STRIDE
     rows = cells * width
@@ -52,9 +52,6 @@
 
     def member(offset):
         return members[offset % n]
-
-    def place_of(t):
-        return 2 * t - 1 if 0 < t <= half else 2 * ((n - t) % n)
 
     sibling = 2 * chip + 1 - core
     barrier = pltpu.get_barrier_semaphore()
@@ -143,7 +140,6 @@
         angle = 2.0 * math.pi * (turns - jnp.floor(turns))
         turn[f] = jnp.cos(angle) / nk
         turn[cells + f] = sign * jnp.sin(angle) / nk
-    wide = (columns + LANES - 1) // LANES * LANES
     column = lax.broadcasted_iota(jnp.int32, (width, wide), 1) + ka * columns
     block = functions // blocks
     masks = []
@@ -163,9 +159,10 @@
     own_lane = lax.broadcasted_iota(jnp.int32, (width, 2 * lanes), 1)
     signs = jnp.where(own_lane % lanes < lanes // 2, 1.0, -1.0)
 
-    def overlap(i):
-        both = slots[pl.ds(2 * i, 2)].reshape(4 * width, padded)
-        product = dot(both, sel[...])
+    def product_of(i, h):
+        return dot(slots[pl.ds(2 * i, 2), :, chunks[h]].reshape(4 * width, -1), sel[chunks[h], :])
+
+    def overlap(i, product):
         for side in range(2):
             low = 2 * width * side
             k = 2 * chip_at(wrap(ring - i - 1 if side else ring + i)) + core
@@ -184,12 +181,15 @@
         hit = ((c < width) & (r == a + c)) | ((c >= width) & (r == b + c - width))
         placers.append(jnp.where(hit, 1.0, 0.0).astype(bf16))
 
+    offset = chip * 2 * columns - start
+
     def place(t):
         value = dot(placers[0], slots[t, :, pl.ds(start, window)])
         for g in range(1, bands):
             window_copy(g, t).wait_recv()
             value = value + dot(placers[g], near[g - 1, t])
-        stack[t] = value.astype(bf16)
+        for c in range(2):
+            stack[c, t] = pltpu.roll(value, window - offset - (core if c else 1 - core) * columns, 1)[:, :wide].astype(bf16)
 
     acc[...] = jnp.zeros((rows, 2 * lanes), f32)
     sel_copy.wait()
@@ -208,32 +208,74 @@
                 @pl.when(s < last)
                 def _():
                     ring_copy(side, s + 1, h).start()
+            if h == 0:
+                product = product_of(i, 0)
         spread(2 * s - 1)
 
         @pl.when(s < half)
         def _():
             spread(2 * s)
 
-        overlap(i)
-
+        overlap(i, product + product_of(i, 1))
+
+    theirs = pl.ds(pl.multiple_of((1 - core) * lanes, LANES), lanes)
     acc_copy = pltpu.make_async_remote_copy(
-        src_ref=acc, dst_ref=acc_in, send_sem=one_s.at[1], recv_sem=one_r.at[1],
+        src_ref=acc.at[:, theirs], dst_ref=acc_in, send_sem=one_s.at[1], recv_sem=one_r.at[1],
         device_id=(sibling, band), device_id_type=MESH)
     acc_copy.start()
     acc_copy.wait_recv()
-    packed[0] = acc[:, mine] + acc_in[:, mine]
-
-    def gather_copy(t):
+    packed[0] = acc[:, mine] + acc_in[...]
+
+    def place_at(receiver, source):
+        t = wrap(receiver - source)
+        return jnp.where((t > 0) & (t <= half), 2 * t - 1, jnp.where(t == 0, 0, 2 * (n - t)))
+
+    def ring_of(line, side):
+        return jnp.where(side == 0, line, n - 1 - line)
+
+    def line_at(d):
+        line = jnp.where(row + d >= half, row + d - half, row + d)
+        return jnp.where(line < 0, line + half, line)
+
+    def gather_copy(d):
+        line = line_at(d)
         return pltpu.make_async_remote_copy(
-            src_ref=packed.at[0], dst_ref=packed.at[place_of(t)], send_sem=gat_s.at[t - 1], recv_sem=gat_r.at[t - 1],
-            device_id=(member(t), band), device_id_type=MESH)
-
-    order = sorted(range(1, n), key=lambda t: -min(t, n - t))
-    for t in order:
-        gather_copy(t).start()
-    pl.loop(0, n)(place)
-    for t in order:
-        gather_copy(t).wait_recv()
+            src_ref=packed.at[0], dst_ref=packed.at[place_at(ring_of(line, odd), ring)],
+            send_sem=gat_s.at[d - 1], recv_sem=gat_r.at[d - 1],
+            device_id=(2 * (2 * line + odd) + core, band), device_id_type=MESH)
+
+    def across_copy(d):
+        source = ring_of(line_at(-d), odd)
+        return pltpu.make_async_remote_copy(
+            src_ref=packed.at[place_at(ring, source)], dst_ref=packed.at[place_at(n - 1 - ring, source)],
+            send_sem=gat_s.at[half - 1 + d], recv_sem=gat_r.at[half - 1 + d],
+            device_id=(2 * (chip + 1 - 2 * odd) + core, band), device_id_type=MESH)
+
+    across_copy(0).start()
+    for d in range(1, half):
+        gather_copy(d).start()
+    pl.loop(0, n // 2)(place)
+    for d in range(1, half):
+        gather_copy(d).wait_recv()
+        across_copy(d).start()
+    pl.loop(n // 2, n)(place)
+
+    @pl.loop(1, half + 1)
+    def _(s):
+        for h in range(2):
+            for side in (True, False):
+                @pl.when(s <= steps(side, h))
+                def _():
+                    ring_copy(side, s, h).wait_send()
+
+    @pl.loop(0, n)
+    def _(t):
+        for g in range(1, bands):
+            window_copy(g, t).wait_send()
+
+    acc_copy.wait_send()
+    for d in range(half):
+        across_copy(d).wait_recv()
 
     rotated = lax.broadcasted_iota(jnp.int32, (rows, lanes), 1)
     flip = jnp.where(rotated < lanes // 2, -1.0, 1.0)
@@ -242,43 +284,29 @@
         [jnp.concatenate(real, 1), jnp.concatenate([flip * swap(x) for x in real], 1)], 0)
     high = left.astype(bf16)
     low = (left - high.astype(f32)).astype(bf16)
-    terms = stack[...].reshape(n * lanes, window)
-    result = dot(jnp.concatenate([high, low], 0), terms)
-    result = result[:2 * rows] + result[2 * rows:]
-    offset = chip * 2 * columns - start
-
-    def cut(c):
-        return pltpu.roll(result, window - offset - c * columns, 1)[:, :wide]
-
-    part[...] = cut(1 - core)
+    factors = jnp.concatenate([high, low], 0)
+
+    def part_of(c):
+        value = dot(factors, stack[c].reshape(n * lanes, wide))
+        return value[:2 * rows] + value[2 * rows:]
+
+    part[...] = part_of(0)
     part_copy = pltpu.make_async_remote_copy(
         src_ref=part, dst_ref=part_in, send_sem=one_s.at[2], recv_sem=one_r.at[2],
         device_id=(sibling, band), device_id_type=MESH)
     part_copy.start()
-    kept = cut(core)
+    kept = part_of(1)
     part_copy.wait_recv()
     whole = kept + part_in[...]
     for ri in range(2):
         for f in range(cells):
             spot = (ri * cells + f) * width
-            out[f, ri] = (whole[spot:spot + width] * masks[f])[:, :columns]
-
-    @pl.loop(1, half + 1)
-    def _(s):
-        for h in range(2):
-            for side in (True, False):
-                @pl.when(s <= steps(side, h))
-                def _():
-                    ring_copy(side, s, h).wait_send()
-
-    @pl.loop(0, n)
-    def _(t):
-        for g in range(1, bands):
-            window_copy(g, t).wait_send()
-
-    for t in order:
-        gather_copy(t).wait_send()
-    acc_copy.wait_send()
+            out[f, :, ri, :] = (whole[spot:spot + width] * masks[f])[:, :columns]
+
+    for d in range(1, half):
+        gather_copy(d).wait_send()
+    for d in range(half):
+        across_copy(d).wait_send()
     part_copy.wait_send()
 
 
@@ -300,9 +328,9 @@
         bf16, f32 = jnp.bfloat16, jnp.float32
         dma = pltpu.SemaphoreType.DMA
         operands = (coefficients, class_weight, diff_class, frag_cells, block_pattern)
-        return pl.pallas_call(
+        result = pl.pallas_call(
             functools.partial(kernel, nk, bands, width, occupied, functions, blocks, cells),
-            out_shape=jax.ShapeDtypeStruct((cells, 2, width, columns), f32),
+            out_shape=jax.ShapeDtypeStruct((cells, width, 2, columns), f32),
             in_specs=[hbm] * 5,
             out_specs=pl.BlockSpec(memory_space=pltpu.VMEM),
             scratch_shapes=[
@@ -311,10 +339,10 @@
                 pltpu.VMEM((padded, 2 * lanes), bf16),
                 pltpu.VMEM((n, 2 * width, padded), bf16),
                 pltpu.VMEM((bands - 1, n, 2 * width, window), bf16),
-                pltpu.VMEM((n, lanes, window), bf16),
+                pltpu.VMEM((2, n, lanes, wide), bf16),
                 pltpu.VMEM((2 * cells, n, 2 * lanes), f32),
                 pltpu.VMEM((rows, 2 * lanes), f32),
-                pltpu.VMEM((rows, 2 * lanes), f32),
+                pltpu.VMEM((rows, lanes), f32),
                 pltpu.VMEM((n, rows, lanes), f32),
                 pltpu.VMEM((2 * rows, wide), f32),
                 pltpu.VMEM((2 * rows, wide), f32),
@@ -329,6 +357,7 @@
                 flops=8 * n * width * lanes * padded, bytes_accessed=8 * n * width * padded, transcendentals=0),
             name="exchange",
         )(*operands)
+        return jnp.swapaxes(result, 1, 2)
 
     placed = (P("ka", None, None, None), P(), P(), P(), P())
     return jax.shard_map(

time: 35.3 us -> 36.8 us (1.042)
  Pallas kernels: 33.5 us -> 35.1 us
    pallas_call x1, Pallas kernels: 33.5 us -> 35.1 us  [shards(): pl.pallas_call(functools.partial(kernel, nk, bands, width, occupied, func...]
    pallas_call x1 -> x0, local copies, waits for them, and re-layouts: 1.57 us -> none  [shards(): pl.pallas_call(functools.partial(kernel, nk, bands, width, occupied, func...]
    unnamed x0 -> x1, local copies, waits for them, and re-layouts: none -> 1.53 us
where the time goes in v4:
time: 36.8 us; the launch traced here: 36.6 us
  Pallas kernels  35.1 us (95%)
  local copies, waits for them, and re-layouts  1.53 us (4%)
    pallas_call x1, Pallas kernels, shards(): pl.pallas_call(functools.partial(kernel, nk, bands, width, occupied, func...  35.1 us
    unnamed x1, local copies, waits for them, and re-layouts  1.53 us

profile of v4, /device:TPU:0, one launch (start us, length us, event | category | flops | bytes accessed | tf_op | source)
XLA Modules:
  0.0 36.6 jit_solution(1921498409510404985)
XLA Ops:
  0.0 35.1 %exchange.1 = f32[2,20,2,150]{3,2,1,0:T(2,128)} custom-call(bf16[1,2,40,2400]{3,2,1,0:T(8,128)(2,1)} %own_hbm.1, f32[16]{0:T(128)} %weight_hbm.1, s32[16,16]{1,0:T(8,128)} %classes_hbm.1, s32[2]{0:T(128)} %frag_hbm.1, s32[2,30]{1,0:T(2,128)} %pattern_hbm.1), custom_call_target="tpu_custom_call" | custom-call | flops 398458880 | bytes 3112960 | tf_op jit(solution)/shard_map/exchange/pallas_call | solution.py:331
  35.1 1.5 %copy.7 = f32[2,2,20,150]{3,1,2,0:T(2,128)} copy(f32[2,2,20,150]{3,1,2,0:T(2,128)} %bitcast.1) | data formatting | bytes 96000

commit v5 on v4

--- a/solution.py
+++ b/solution.py
@@ -218,6 +218,11 @@
 
         overlap(i, product + product_of(i, 1))
 
+        @pl.when(i > 0)
+        def _():
+            place(2 * i - 2)
+            place(2 * i - 1)
+
     theirs = pl.ds(pl.multiple_of((1 - core) * lanes, LANES), lanes)
     acc_copy = pltpu.make_async_remote_copy(
         src_ref=acc.at[:, theirs], dst_ref=acc_in, send_sem=one_s.at[1], recv_sem=one_r.at[1],
@@ -226,39 +231,19 @@
     acc_copy.wait_recv()
     packed[0] = acc[:, mine] + acc_in[...]
 
-    def place_at(receiver, source):
-        t = wrap(receiver - source)
-        return jnp.where((t > 0) & (t <= half), 2 * t - 1, jnp.where(t == 0, 0, 2 * (n - t)))
-
-    def ring_of(line, side):
-        return jnp.where(side == 0, line, n - 1 - line)
-
-    def line_at(d):
-        line = jnp.where(row + d >= half, row + d - half, row + d)
-        return jnp.where(line < 0, line + half, line)
-
-    def gather_copy(d):
-        line = line_at(d)
+    def place_of(t):
+        return 2 * t - 1 if 0 < t <= half else 2 * ((n - t) % n)
+
+    def gather_copy(t):
         return pltpu.make_async_remote_copy(
-            src_ref=packed.at[0], dst_ref=packed.at[place_at(ring_of(line, odd), ring)],
-            send_sem=gat_s.at[d - 1], recv_sem=gat_r.at[d - 1],
-            device_id=(2 * (2 * line + odd) + core, band), device_id_type=MESH)
-
-    def across_copy(d):
-        source = ring_of(line_at(-d), odd)
-        return pltpu.make_async_remote_copy(
-            src_ref=packed.at[place_at(ring, source)], dst_ref=packed.at[place_at(n - 1 - ring, source)],
-            send_sem=gat_s.at[half - 1 + d], recv_sem=gat_r.at[half - 1 + d],
-            device_id=(2 * (chip + 1 - 2 * odd) + core, band), device_id_type=MESH)
-
-    across_copy(0).start()
-    for d in range(1, half):
-        gather_copy(d).start()
-    pl.loop(0, n // 2)(place)
-    for d in range(1, half):
-        gather_copy(d).wait_recv()
-        across_copy(d).start()
-    pl.loop(n // 2, n)(place)
+            src_ref=packed.at[0], dst_ref=packed.at[place_of(t)], send_sem=gat_s.at[t - 1], recv_sem=gat_r.at[t - 1],
+            device_id=(member(t), band), device_id_type=MESH)
+
+    order = sorted(range(1, n), key=lambda t: -min(t, n - t))
+    for t in order:
+        gather_copy(t).start()
+    place(n - 2)
+    place(n - 1)
 
     @pl.loop(1, half + 1)
     def _(s):
@@ -274,8 +259,8 @@
             window_copy(g, t).wait_send()
 
     acc_copy.wait_send()
-    for d in range(half):
-        across_copy(d).wait_recv()
+    for t in order:
+        gather_copy(t).wait_recv()
 
     rotated = lax.broadcasted_iota(jnp.int32, (rows, lanes), 1)
     flip = jnp.where(rotated < lanes // 2, -1.0, 1.0)
@@ -301,12 +286,10 @@
     for ri in range(2):
         for f in range(cells):
             spot = (ri * cells + f) * width
-            out[f, :, ri, :] = (whole[spot:spot + width] * masks[f])[:, :columns]
-
-    for d in range(1, half):
-        gather_copy(d).wait_send()
-    for d in range(half):
-        across_copy(d).wait_send()
+            out[f, ri] = (whole[spot:spot + width] * masks[f])[:, :columns]
+
+    for t in order:
+        gather_copy(t).wait_send()
     part_copy.wait_send()
 
 
@@ -328,9 +311,9 @@
         bf16, f32 = jnp.bfloat16, jnp.float32
         dma = pltpu.SemaphoreType.DMA
         operands = (coefficients, class_weight, diff_class, frag_cells, block_pattern)
-        result = pl.pallas_call(
+        return pl.pallas_call(
             functools.partial(kernel, nk, bands, width, occupied, functions, blocks, cells),
-            out_shape=jax.ShapeDtypeStruct((cells, width, 2, columns), f32),
+            out_shape=jax.ShapeDtypeStruct((cells, 2, width, columns), f32),
             in_specs=[hbm] * 5,
             out_specs=pl.BlockSpec(memory_space=pltpu.VMEM),
             scratch_shapes=[
@@ -357,7 +340,6 @@
                 flops=8 * n * width * lanes * padded, bytes_accessed=8 * n * width * padded, transcendentals=0),
             name="exchange",
         )(*operands)
-        return jnp.swapaxes(result, 1, 2)
 
     placed = (P("ka", None, None, None), P(), P(), P(), P())
     return jax.shard_map(

time: 36.8 us -> 35.7 us (0.970)
  Pallas kernels: 35.1 us -> 33.9 us
    pallas_call x0 -> x1, local copies, waits for them, and re-layouts: none -> 1.57 us  [shards(): pl.pallas_call(functools.partial(kernel, nk, bands, width, occupied, func...]
    unnamed x1 -> x0, local copies, waits for them, and re-layouts: 1.53 us -> none
    pallas_call x1, Pallas kernels: 35.1 us -> 33.9 us  [shards(): pl.pallas_call(functools.partial(kernel, nk, bands, width, occupied, func...]
where the time goes in v5:
time: 35.7 us; the launch traced here: 35.5 us
  Pallas kernels  33.9 us (95%)
  local copies, waits for them, and re-layouts  1.57 us (4%)
    pallas_call x1, Pallas kernels, shards(): pl.pallas_call(functools.partial(kernel, nk, bands, width, occupied, func...  33.9 us
    pallas_call x1, local copies, waits for them, and re-layouts, shards(): pl.pallas_call(functools.partial(kernel, nk, bands, width, occupied, func...  1.57 us

profile of v5, /device:TPU:0, one launch (start us, length us, event | category | flops | bytes accessed | tf_op | source)
XLA Modules:
  0.0 35.5 jit_solution(12614476671493292825)
XLA Ops:
  0.0 33.9 %exchange.1 = f32[2,2,20,150]{3,2,1,0:T(8,128)} custom-call(bf16[1,2,40,2400]{3,2,1,0:T(8,128)(2,1)} %own_hbm.1, f32[16]{0:T(128)} %weight_hbm.1, s32[16,16]{1,0:T(8,128)} %classes_hbm.1, s32[2]{0:T(128)} %frag_hbm.1, s32[2,30]{1,0:T(2,128)} %pattern_hbm.1), custom_call_target="tpu_custom_call" | custom-call | flops 398458880 | bytes 3112960 | tf_op jit(solution)/shard_map/exchange/pallas_call | solution.py:314
  33.9 1.6 %copy.6 = f32[2,2,20,150]{3,1,2,0:T(2,128)} copy(f32[2,2,20,150]{3,2,1,0:T(8,128)} %exchange.1) | data formatting | bytes 96000 | tf_op jit(solution)/shard_map/exchange/pallas_call | solution.py:314

commit v6 on v5

--- a/solution.py
+++ b/solution.py
@@ -55,7 +55,7 @@
 
     sibling = 2 * chip + 1 - core
     barrier = pltpu.get_barrier_semaphore()
-    for offset in range(1, n):
+    for offset in (1, -1):
         pl.semaphore_signal(barrier, inc=1, device_id=(member(offset), band), device_id_type=MESH)
     pl.semaphore_signal(barrier, inc=1, device_id=(sibling, band), device_id_type=MESH)
     for offset in range(1, bands):
@@ -76,7 +76,7 @@
     re, im = own[0, 0], own[0, 1]
     slots[0, :, :functions] = (dot(pick_re, re) + dot(pick_im, im)).astype(bf16)
 
-    pl.semaphore_wait(barrier, n - 1 + 1 + bands - 1)
+    pl.semaphore_wait(barrier, 2 + 1 + bands - 1)
 
     def ring_copy(to_right, s, h):
         if to_right:
@@ -140,16 +140,6 @@
         angle = 2.0 * math.pi * (turns - jnp.floor(turns))
         turn[f] = jnp.cos(angle) / nk
         turn[cells + f] = sign * jnp.sin(angle) / nk
-    column = lax.broadcasted_iota(jnp.int32, (width, wide), 1) + ka * columns
-    block = functions // blocks
-    masks = []
-    for f in range(cells):
-        mask = jnp.zeros((width, wide), f32)
-        for i in range(blocks):
-            keep = (column >= i * block) & (column < (i + 1) * block)
-            mask = jnp.where(keep, pattern[f, i].astype(f32), mask)
-        masks.append(mask)
-
     def swap(x):
         return pltpu.roll(x, lanes // 2, 1)
 
@@ -192,7 +182,6 @@
             stack[c, t] = pltpu.roll(value, window - offset - (core if c else 1 - core) * columns, 1)[:, :wide].astype(bf16)
 
     acc[...] = jnp.zeros((rows, 2 * lanes), f32)
-    sel_copy.wait()
 
     @pl.loop(0, half)
     def _(i):
@@ -209,6 +198,10 @@
                 def _():
                     ring_copy(side, s + 1, h).start()
             if h == 0:
+                @pl.when(i == 0)
+                def _():
+                    sel_copy.wait()
+
                 product = product_of(i, 0)
         spread(2 * s - 1)
 
@@ -244,6 +237,16 @@
         gather_copy(t).start()
     place(n - 2)
     place(n - 1)
+
+    column = lax.broadcasted_iota(jnp.int32, (width, wide), 1) + ka * columns
+    block = functions // blocks
+    masks = []
+    for f in range(cells):
+        mask = jnp.zeros((width, wide), f32)
+        for i in range(blocks):
+            keep = (column >= i * block) & (column < (i + 1) * block)
+            mask = jnp.where(keep, pattern[f, i].astype(f32), mask)
+        masks.append(mask)
 
     @pl.loop(1, half + 1)
     def _(s):

time: 35.7 us -> 35.3 us (0.989)
  Pallas kernels: 33.9 us -> 33.5 us
    pallas_call x1, Pallas kernels: 33.9 us -> 33.5 us  [shards(): pl.pallas_call(functools.partial(kernel, nk, bands, width, occupied, func...]
where the time goes in v6:
time: 35.3 us; the launch traced here: 35.1 us
  Pallas kernels  33.5 us (95%)
  local copies, waits for them, and re-layouts  1.57 us (4%)
    pallas_call x1, Pallas kernels, shards(): pl.pallas_call(functools.partial(kernel, nk, bands, width, occupied, func...  33.5 us
    pallas_call x1, local copies, waits for them, and re-layouts, shards(): pl.pallas_call(functools.partial(kernel, nk, bands, width, occupied, func...  1.57 us

profile of v6, /device:TPU:0, one launch (start us, length us, event | category | flops | bytes accessed | tf_op | source)
XLA Modules:
  0.0 35.1 jit_solution(14499640550766895636)
XLA Ops:
  0.0 33.5 %exchange.1 = f32[2,2,20,150]{3,2,1,0:T(8,128)} custom-call(bf16[1,2,40,2400]{3,2,1,0:T(8,128)(2,1)} %own_hbm.1, f32[16]{0:T(128)} %weight_hbm.1, s32[16,16]{1,0:T(8,128)} %classes_hbm.1, s32[2]{0:T(128)} %frag_hbm.1, s32[2,30]{1,0:T(2,128)} %pattern_hbm.1), custom_call_target="tpu_custom_call" | custom-call | flops 398458880 | bytes 3112960 | tf_op jit(solution)/shard_map/exchange/pallas_call | solution.py:317
  33.6 1.6 %copy.6 = f32[2,2,20,150]{3,1,2,0:T(2,128)} copy(f32[2,2,20,150]{3,2,1,0:T(8,128)} %exchange.1) | data formatting | bytes 96000 | tf_op jit(solution)/shard_map/exchange/pallas_call | solution.py:317

commit v7 on v4

--- a/solution.py
+++ b/solution.py
@@ -55,7 +55,7 @@
 
     sibling = 2 * chip + 1 - core
     barrier = pltpu.get_barrier_semaphore()
-    for offset in range(1, n):
+    for offset in (1, -1):
         pl.semaphore_signal(barrier, inc=1, device_id=(member(offset), band), device_id_type=MESH)
     pl.semaphore_signal(barrier, inc=1, device_id=(sibling, band), device_id_type=MESH)
     for offset in range(1, bands):
@@ -76,7 +76,7 @@
     re, im = own[0, 0], own[0, 1]
     slots[0, :, :functions] = (dot(pick_re, re) + dot(pick_im, im)).astype(bf16)
 
-    pl.semaphore_wait(barrier, n - 1 + 1 + bands - 1)
+    pl.semaphore_wait(barrier, 2 + 1 + bands - 1)
 
     def ring_copy(to_right, s, h):
         if to_right:
@@ -140,16 +140,6 @@
         angle = 2.0 * math.pi * (turns - jnp.floor(turns))
         turn[f] = jnp.cos(angle) / nk
         turn[cells + f] = sign * jnp.sin(angle) / nk
-    column = lax.broadcasted_iota(jnp.int32, (width, wide), 1) + ka * columns
-    block = functions // blocks
-    masks = []
-    for f in range(cells):
-        mask = jnp.zeros((width, wide), f32)
-        for i in range(blocks):
-            keep = (column >= i * block) & (column < (i + 1) * block)
-            mask = jnp.where(keep, pattern[f, i].astype(f32), mask)
-        masks.append(mask)
-
     def swap(x):
         return pltpu.roll(x, lanes // 2, 1)
 
@@ -192,7 +182,6 @@
             stack[c, t] = pltpu.roll(value, window - offset - (core if c else 1 - core) * columns, 1)[:, :wide].astype(bf16)
 
     acc[...] = jnp.zeros((rows, 2 * lanes), f32)
-    sel_copy.wait()
 
     @pl.loop(0, half)
     def _(i):
@@ -209,6 +198,10 @@
                 def _():
                     ring_copy(side, s + 1, h).start()
             if h == 0:
+                @pl.when(i == 0)
+                def _():
+                    sel_copy.wait()
+
                 product = product_of(i, 0)
         spread(2 * s - 1)
 
@@ -217,6 +210,11 @@
             spread(2 * s)
 
         overlap(i, product + product_of(i, 1))
+
+        @pl.when(i > 0)
+        def _():
+            place(2 * i - 2)
+            place(2 * i - 1)
 
     theirs = pl.ds(pl.multiple_of((1 - core) * lanes, LANES), lanes)
     acc_copy = pltpu.make_async_remote_copy(
@@ -254,11 +252,21 @@
     across_copy(0).start()
     for d in range(1, half):
         gather_copy(d).start()
-    pl.loop(0, n // 2)(place)
     for d in range(1, half):
         gather_copy(d).wait_recv()
         across_copy(d).start()
-    pl.loop(n // 2, n)(place)
+    place(n - 2)
+    place(n - 1)
+
+    column = lax.broadcasted_iota(jnp.int32, (width, wide), 1) + ka * columns
+    block = functions // blocks
+    masks = []
+    for f in range(cells):
+        mask = jnp.zeros((width, wide), f32)
+        for i in range(blocks):
+            keep = (column >= i * block) & (column < (i + 1) * block)
+            mask = jnp.where(keep, pattern[f, i].astype(f32), mask)
+        masks.append(mask)
 
     @pl.loop(1, half + 1)
     def _(s):
@@ -301,7 +309,7 @@
     for ri in range(2):
         for f in range(cells):
             spot = (ri * cells + f) * width
-            out[f, :, ri, :] = (whole[spot:spot + width] * masks[f])[:, :columns]
+            out[f, ri] = (whole[spot:spot + width] * masks[f])[:, :columns]
 
     for d in range(1, half):
         gather_copy(d).wait_send()
@@ -328,9 +336,9 @@
         bf16, f32 = jnp.bfloat16, jnp.float32
         dma = pltpu.SemaphoreType.DMA
         operands = (coefficients, class_weight, diff_class, frag_cells, block_pattern)
-        result = pl.pallas_call(
+        return pl.pallas_call(
             functools.partial(kernel, nk, bands, width, occupied, functions, blocks, cells),
-            out_shape=jax.ShapeDtypeStruct((cells, width, 2, columns), f32),
+            out_shape=jax.ShapeDtypeStruct((cells, 2, width, columns), f32),
             in_specs=[hbm] * 5,
             out_specs=pl.BlockSpec(memory_space=pltpu.VMEM),
             scratch_shapes=[
@@ -357,7 +365,6 @@
                 flops=8 * n * width * lanes * padded, bytes_accessed=8 * n * width * padded, transcendentals=0),
             name="exchange",
         )(*operands)
-        return jnp.swapaxes(result, 1, 2)
 
     placed = (P("ka", None, None, None), P(), P(), P(), P())
     return jax.shard_map(

time: 36.8 us -> 36.6 us (level)
    pallas_call x0 -> x1, local copies, waits for them, and re-layouts: none -> 1.57 us  [shards(): pl.pallas_call(functools.partial(kernel, nk, bands, width, occupied, func...]
    unnamed x1 -> x0, local copies, waits for them, and re-layouts: 1.53 us -> none
where the time goes in v7:
time: 36.6 us; the launch traced here: 36.5 us
  Pallas kernels  34.9 us (95%)
  local copies, waits for them, and re-layouts  1.57 us (4%)
    pallas_call x1, Pallas kernels, shards(): pl.pallas_call(functools.partial(kernel, nk, bands, width, occupied, func...  34.9 us
    pallas_call x1, local copies, waits for them, and re-layouts, shards(): pl.pallas_call(functools.partial(kernel, nk, bands, width, occupied, func...  1.57 us

profile of v7, /device:TPU:0, one launch (start us, length us, event | category | flops | bytes accessed | tf_op | source)
XLA Modules:
  0.0 36.5 jit_solution(13857012140895494022)
XLA Ops:
  0.0 34.9 %exchange.1 = f32[2,2,20,150]{3,2,1,0:T(8,128)} custom-call(bf16[1,2,40,2400]{3,2,1,0:T(8,128)(2,1)} %own_hbm.1, f32[16]{0:T(128)} %weight_hbm.1, s32[16,16]{1,0:T(8,128)} %classes_hbm.1, s32[2]{0:T(128)} %frag_hbm.1, s32[2,30]{1,0:T(2,128)} %pattern_hbm.1), custom_call_target="tpu_custom_call" | custom-call | flops 398458880 | bytes 3112960 | tf_op jit(solution)/shard_map/exchange/pallas_call | solution.py:339
  34.9 1.6 %copy.6 = f32[2,2,20,150]{3,1,2,0:T(2,128)} copy(f32[2,2,20,150]{3,2,1,0:T(8,128)} %exchange.1) | data formatting | bytes 96000 | tf_op jit(solution)/shard_map/exchange/pallas_call | solution.py:339

commit v8 on v6

--- a/solution.py
+++ b/solution.py
@@ -10,6 +10,7 @@
 
 MESH = pl.DeviceIdType.MESH
 LANES = 128
+CHUNKS = 4
 STRIDE = 32
 
 
@@ -24,8 +25,10 @@
     chip, core = ka // 2, ka % 2
     padded = slots.shape[2]
     tiles = padded // LANES
-    first = (tiles + 1) // 2 * LANES
-    chunks = (pl.ds(0, first), pl.ds(first, padded - first))
+    ends = [(tiles * h + CHUNKS - 1) // CHUNKS * LANES for h in range(CHUNKS + 1)]
+    chunks = [pl.ds(ends[h], ends[h + 1] - ends[h]) for h in range(CHUNKS)]
+    middle = ends[CHUNKS // 2]
+    halves = (pl.ds(0, middle), pl.ds(middle, padded - middle))
     window, wide = near.shape[3], stack.shape[3]
     columns = functions // nk
     lanes = 2 * bands * STRIDE
@@ -89,8 +92,11 @@
             send_sem=ss.at[s - 1, h], recv_sem=rs.at[s - 1, h],
             device_id=(to, band), device_id_type=MESH)
 
+    def turn_of(to_right, h):
+        return h if to_right else (h + CHUNKS // 2) % CHUNKS
+
     def steps(to_right, h):
-        return half if h == (0 if to_right else 1) else half - 1
+        return half if (h < CHUNKS // 2) == to_right else half - 1
 
     start = pl.multiple_of(jnp.minimum(chip * 2 * columns // LANES, tiles - window // LANES) * LANES, LANES)
 
@@ -104,9 +110,9 @@
         for g in range(1, bands):
             window_copy(g, t).start()
 
-    for h in range(2):
+    for h in range(CHUNKS):
         for side in (True, False):
-            ring_copy(side, 1, h).start()
+            ring_copy(side, 1, turn_of(side, h)).start()
     spread(0)
 
     r, c = iotas((occupied, lanes))
@@ -150,7 +156,7 @@
     signs = jnp.where(own_lane % lanes < lanes // 2, 1.0, -1.0)
 
     def product_of(i, h):
-        return dot(slots[pl.ds(2 * i, 2), :, chunks[h]].reshape(4 * width, -1), sel[chunks[h], :])
+        return dot(slots[pl.ds(2 * i, 2), :, halves[h]].reshape(4 * width, -1), sel[halves[h], :])
 
     def overlap(i, product):
         for side in range(2):
@@ -186,18 +192,19 @@
     @pl.loop(0, half)
     def _(i):
         s = i + 1
-        for h in range(2):
+        for h in range(CHUNKS):
             for side in (True, False):
-                last = steps(side, h)
+                chunk = turn_of(side, h)
+                last = steps(side, chunk)
 
                 @pl.when(s <= last)
                 def _():
-                    ring_copy(side, s, h).wait_recv()
+                    ring_copy(side, s, chunk).wait_recv()
 
                 @pl.when(s < last)
                 def _():
-                    ring_copy(side, s + 1, h).start()
-            if h == 0:
+                    ring_copy(side, s + 1, chunk).start()
+            if h == CHUNKS // 2 - 1:
                 @pl.when(i == 0)
                 def _():
                     sel_copy.wait()
@@ -250,7 +257,7 @@
 
     @pl.loop(1, half + 1)
     def _(s):
-        for h in range(2):
+        for h in range(CHUNKS):
             for side in (True, False):
                 @pl.when(s <= steps(side, h))
                 def _():
@@ -333,7 +340,7 @@
                 pltpu.VMEM((2 * rows, wide), f32),
                 pltpu.VMEM((2 * rows, wide), f32),
                 dma((5,)),
-                dma((n // 2, 2)), dma((n // 2, 2)), dma((n // 2, 2)), dma((n // 2, 2)),
+                *[dma((n // 2, CHUNKS))] * 4,
                 dma((bands - 1, n)), dma((bands - 1, n)),
                 dma((n - 1,)), dma((n - 1,)), dma((3,)), dma((3,)),
             ],

time: 35.3 us -> 34.6 us (0.980)
  Pallas kernels: 33.5 us -> 32.8 us
    pallas_call x1, Pallas kernels: 33.5 us -> 32.8 us  [shards(): pl.pallas_call(functools.partial(kernel, nk, bands, width, occupied, func...]
where the time goes in v8:
time: 34.6 us; the launch traced here: 34.4 us
  Pallas kernels  32.8 us (95%)
  local copies, waits for them, and re-layouts  1.57 us (5%)
    pallas_call x1, Pallas kernels, shards(): pl.pallas_call(functools.partial(kernel, nk, bands, width, occupied, func...  32.8 us
    pallas_call x1, local copies, waits for them, and re-layouts, shards(): pl.pallas_call(functools.partial(kernel, nk, bands, width, occupied, func...  1.57 us

profile of v8, /device:TPU:0, one launch (start us, length us, event | category | flops | bytes accessed | tf_op | source)
XLA Modules:
  0.0 34.4 jit_solution(15026452195437572489)
XLA Ops:
  0.0 32.8 %exchange.1 = f32[2,2,20,150]{3,2,1,0:T(8,128)} custom-call(bf16[1,2,40,2400]{3,2,1,0:T(8,128)(2,1)} %own_hbm.1, f32[16]{0:T(128)} %weight_hbm.1, s32[16,16]{1,0:T(8,128)} %classes_hbm.1, s32[2]{0:T(128)} %frag_hbm.1, s32[2,30]{1,0:T(2,128)} %pattern_hbm.1), custom_call_target="tpu_custom_call" | custom-call | flops 398458880 | bytes 3112960 | tf_op jit(solution)/shard_map/exchange/pallas_call | solution.py:324
  32.8 1.6 %copy.6 = f32[2,2,20,150]{3,1,2,0:T(2,128)} copy(f32[2,2,20,150]{3,2,1,0:T(8,128)} %exchange.1) | data formatting | bytes 96000 | tf_op jit(solution)/shard_map/exchange/pallas_call | solution.py:324

commit v9 on v8

--- a/solution.py
+++ b/solution.py
@@ -10,7 +10,7 @@
 
 MESH = pl.DeviceIdType.MESH
 LANES = 128
-CHUNKS = 4
+CHUNKS = 6
 STRIDE = 32
 
 

time: 34.6 us -> 34.8 us (level)
  no operation moved by 1% of the time
where the time goes in v9:
time: 34.8 us; the launch traced here: 34.7 us
  Pallas kernels  33.1 us (95%)
  local copies, waits for them, and re-layouts  1.57 us (5%)
    pallas_call x1, Pallas kernels, shards(): pl.pallas_call(functools.partial(kernel, nk, bands, width, occupied, func...  33.1 us
    pallas_call x1, local copies, waits for them, and re-layouts, shards(): pl.pallas_call(functools.partial(kernel, nk, bands, width, occupied, func...  1.57 us

profile of v9, /device:TPU:0, one launch (start us, length us, event | category | flops | bytes accessed | tf_op | source)
XLA Modules:
  0.0 34.7 jit_solution(5876489401516001109)
XLA Ops:
  0.0 33.1 %exchange.1 = f32[2,2,20,150]{3,2,1,0:T(8,128)} custom-call(bf16[1,2,40,2400]{3,2,1,0:T(8,128)(2,1)} %own_hbm.1, f32[16]{0:T(128)} %weight_hbm.1, s32[16,16]{1,0:T(8,128)} %classes_hbm.1, s32[2]{0:T(128)} %frag_hbm.1, s32[2,30]{1,0:T(2,128)} %pattern_hbm.1), custom_call_target="tpu_custom_call" | custom-call | flops 398458880 | bytes 3112960 | tf_op jit(solution)/shard_map/exchange/pallas_call | solution.py:324
  33.1 1.6 %copy.6 = f32[2,2,20,150]{3,1,2,0:T(2,128)} copy(f32[2,2,20,150]{3,2,1,0:T(8,128)} %exchange.1) | data formatting | bytes 96000 | tf_op jit(solution)/shard_map/exchange/pallas_call | solution.py:324
